TPU v7x, 256 devices: a whole 4x4x8 slice. The times are simulated.
256 devices in a mesh: dp: 64 (over z, x_lo, y), mp: 4 (over x_hi, core).
Axes of the slice: x: 4 (x_hi: 2, x_lo: 2; x = x_hi * 2 + x_lo), y: 4, z: 8, core: 2. Of those that a mesh axis runs over, the one named last changes fastest.
Arguments:
- image_feats: bfloat16 [14336, 1152], P('dp'), may hold values from -6 to 6
- text_feats: bfloat16 [14336, 1152], P('dp'), may hold values from -6 to 6
- image_proj: bfloat16 [1152, 1152], P(None, 'mp'), may hold values from -0.1875 to 0.1875
- text_proj: bfloat16 [1152, 1152], P(None, 'mp'), may hold values from -0.1875 to 0.1875
- log_temp: float32 [1], replicated, may hold values from 1 to 2.3
- bias: float32 [1], replicated, may hold values from -4 to -1
Outputs:
- image_proj_grad: float32 [1152, 1152], P('dp', 'mp')
- text_proj_grad: float32 [1152, 1152], P('dp', 'mp')
All inputs are finite; a program needn't handle non-finite values.
Results may differ from a plain program's by a relative error of at most 0.004.
Values may be sent and summed in bfloat16 or wider, within the bound.
A program may use at most 64 MiB of HBM per device.

v0:
```python
import jax
import jax.numpy as jnp
from jax import lax
from jax.sharding import PartitionSpec as P


def unit_rows(emb):
    wide = emb.astype(jnp.float32)
    scale = lax.rsqrt(jnp.sum(wide * wide, axis=1, keepdims=True) + 1e-06)
    return (wide * scale, scale)


def contract_rows(left, right):
    return lax.dot_general(
        left, right, (((0,), (0,)), ((), ())), preferred_element_type=jnp.float32
    )


def local(image_feats, text_feats, image_proj, text_proj, log_temp, bias):
    rows = image_feats.shape[0]
    width_part = image_proj.shape[1]
    cycle_size = lax.axis_size("dp")
    mp_index = lax.axis_index("mp")
    total = rows * cycle_size
    image_emb = jnp.dot(image_feats, image_proj, preferred_element_type=jnp.float32).astype(
        jnp.bfloat16
    )
    text_emb = jnp.dot(text_feats, text_proj, preferred_element_type=jnp.float32).astype(
        jnp.bfloat16
    )
    image_full = lax.all_gather(image_emb, "mp", axis=1, tiled=True)
    text_mine = lax.all_to_all(text_emb, "mp", split_axis=0, concat_axis=1, tiled=True)
    quarter = text_mine.shape[0]
    image_unit, image_scale = unit_rows(image_full)
    text_unit, text_scale = unit_rows(text_mine)
    image_x = image_unit.astype(jnp.bfloat16)
    text_x = text_unit.astype(jnp.bfloat16)
    temp = jnp.exp(log_temp[0])
    shift = bias[0]
    row_ids = lax.axis_index("dp") * rows + jnp.arange(rows)
    piece = lax.all_gather(text_x, "dp", axis=0, tiled=True)
    count = piece.shape[0]
    places = jnp.arange(count)
    col_ids = places // quarter * rows + mp_index * quarter + places % quarter
    dots = lax.dot_general(
        image_x, piece, (((1,), (1,)), ((), ())), preferred_element_type=jnp.float32
    )
    logits = temp * dots + shift
    sign = jnp.where(row_ids[:, None] == col_ids[None, :], jnp.float32(1.0), jnp.float32(-1.0))
    grad = -sign * jax.nn.sigmoid(-sign * logits) / total
    scaled = (temp * grad).astype(jnp.bfloat16)
    image_dx = jnp.dot(scaled, piece, preferred_element_type=jnp.float32)
    scaled, piece_dx = (scaled, image_dx)
    text_all = contract_rows(scaled, image_x)
    image_dx, text_all = (piece_dx, text_all)
    text_dx = lax.psum_scatter(text_all, "dp", scatter_dimension=0, tiled=True)
    summed = lax.psum(image_dx, "mp")
    inner = jnp.sum(image_unit * summed, axis=1, keepdims=True)
    full_dz = image_scale * (summed - image_unit * inner)
    image_dz = lax.dynamic_slice_in_dim(full_dz, mp_index * width_part, width_part, 1).astype(
        jnp.bfloat16
    )
    text_inner = jnp.sum(text_unit * text_dx, axis=1, keepdims=True)
    text_dz = (text_scale * (text_dx - text_unit * text_inner)).astype(jnp.bfloat16)
    text_back = lax.all_to_all(text_dz, "mp", split_axis=1, concat_axis=0, tiled=True)
    image_part = contract_rows(image_feats, image_dz)
    text_part = contract_rows(text_feats, text_back)
    image_proj_grad, text_proj_grad = (
        lax.psum_scatter(image_part, "dp", scatter_dimension=0, tiled=True),
        lax.psum_scatter(text_part, "dp", scatter_dimension=0, tiled=True),
    )
    return (image_proj_grad, text_proj_grad)


def solution(mesh):
    placed = (P("dp", None), P("dp", None), P(None, "mp"), P(None, "mp"), P(), P())
    return jax.shard_map(
        local, mesh=mesh, in_specs=placed, out_specs=(P("dp", "mp"), P("dp", "mp")), check_vma=False
    )
```

profile of v0, /device:TPU:2, one launch (start us, length us, event | category | flops | bytes accessed | tf_op | source)
XLA Modules:
  0.0 1370.0 jit_solution(10936195650981002592)
XLA Ops:
  7.2 0.0 copy-start
  7.2 0.0 all-gather.2.cloned.1.call-start
  7.2 1.0 copy-done
  8.3 1.4 convolution_convert_fusion
  9.7 0.0 copy-start.2
  9.7 0.0 copy-start.4
  9.7 0.1 copy.23
  9.9 9.9 all_to_all.32
  19.8 0.1 copy.24
  19.9 0.2 reshape.51
  20.1 0.1 fusion.14
  20.2 0.8 multiply_convert_fusion.1
  21.0 0.0 all-gather.2.cloned.1.call-update
  21.0 0.0 all-reduce.7.cloned.1.call-start
  22.5 0.0 copy-done.2
  22.5 0.0 copy-done.4
  22.5 0.4 convolution_convert_fusion.1
  22.9 8.7 all_gather.6
  31.6 0.2 fusion.9
  31.8 299.6 %all-gather.2.cloned.1.call-done = bf16[3584,1152]{1,0:T(8,128)(2,1)} async-done(((bf16[56,1152]{1,0:T(8,128)(2,1)}), bf16[3584,1152]{1,0:T(8,128)(2,1)}) %all-gather.2.cloned.1.call-update) | async-done | bytes 8257552 | tf_op jit(solution)/shard_map/all_gather | solution.py:41
  331.3 7.5 fusion.8
  338.9 1.2 copy-done.3
  340.0 4.5 fusion.31
  344.5 0.0 all-reduce.7.cloned.1.call-update
  344.6 0.2 reduce-scatter.7.cloned.1.call-start
  344.8 9.7 fusion.11
  354.5 0.0 reduce-scatter.7.cloned.1.call-update
  354.5 42.0 %all-reduce.7.cloned.1.call-done = f32[224,1152]{0,1:T(8,128)} async-done(((f32[224,1152]{0,1:T(8,128)}), f32[224,1152]{0,1:T(8,128)}) %all-reduce.7.cloned.1.call-update) | async-done | bytes 1032208 | tf_op jit(solution)/shard_map/psum | solution.py:57
  396.5 1.5 multiply_reduce_fusion
  398.0 348.1 %reduce-scatter.7.cloned.1.call-done = f32[56,1152]{1,0:T(8,128)} async-done(((f32[3584,1152]{1,0:T(8,128)}), f32[56,1152]{1,0:T(8,128)}) %reduce-scatter.7.cloned.1.call-update) | async-done | bytes 258064
  746.1 1.1 multiply_reduce_fusion.1
  747.2 1.1 multiply_convert_fusion
  748.3 0.2 all_to_all.26
  748.5 0.0 copy-start.1
  748.5 0.7 copy.26
  749.2 3.3 all-to-all-start.1
  752.6 0.0 all-reduce.9.cloned.1.call-start
  752.6 2.4 convolution_bitcast_fusion.1
  755.0 4.1 all-to-all-done.1
  759.1 0.0 copy-done.1
  759.1 1.4 convolution_bitcast_fusion
  760.6 0.0 all-reduce.9.cloned.1.call-update
  760.6 0.6 copy-done.6
  761.2 0.6 dynamic-slice
  762.5 598.3 %all-reduce.9.cloned.1.call-done = (f32[1152,288]{0,1:T(8,128)}, f32[1152,288]{0,1:T(8,128)}) async-done(((f32[1152,288]{0,1:T(8,128)}, f32[1152,288]{0,1:T(8,128)}), (f32[1152,288]{0,1:T(8,128)}, f32[1152,288]{0,1:T(8,128)})) %all-reduce.9.cloned.1.call-update) | async-done | bytes 2654224
  1360.8 1.2 constant_dynamic-slice_fusion
  1362.0 0.7 copy.27
  1362.7 0.7 copy.28
  (9 shorter events, 0.1 us)
Async XLA Ops:
  7.2 1.1 copy-start
  7.2 324.2 %all-gather.2.cloned.1.call-start = ((), (), s32[]{:S(2)}) async-start(), calls=%async_computation.3 | async-start | bytes 8386560 | tf_op jit(solution)/shard_map/all_gather | solution.py:41
  9.7 12.8 copy-start.2
  9.7 12.8 copy-start.4
  21.0 375.5 %all-reduce.7.cloned.1.call-start = ((), (), s32[]{:S(2)}) async-start(), calls=%async_computation.4 | async-start | bytes 2359296 | tf_op jit(solution)/shard_map/psum | solution.py:57
  331.3 8.7 copy-start.5
  338.9 1.2 copy-start.3
  344.6 401.5 %reduce-scatter.7.cloned.1.call-start = ((), (), s32[]{:S(2)}) async-start(), calls=%async_computation.5 | async-start | bytes 16773120
  748.5 10.6 copy-start.1
  749.2 9.9 all-to-all-start.1
  752.6 608.2 %all-reduce.9.cloned.1.call-start = ((), (), s32[]{:S(2)}) async-start(), calls=%async_computation.6 | async-start | bytes 5308416
  760.6 0.7 copy-start.6
Sparse Core Ops, SparseCore 0:
  21.2 310.1 all-gather.1
  344.7 51.7 all-reduce.6
  399.1 346.9 reduce-scatter.6
  760.7 600.0 all-reduce.8
where the time goes:
time: 1370 us
  waiting for transfers between devices  1290 us (94%)
  matrix products  27.4 us (2%)
  blocking collectives  18.6 us (1%)
  between operations  15.9 us (1%)
    unnamed x6, waiting for transfers between devices  946 us
    all_gather x1, waiting for transfers between devices, local(): piece = lax.all_gather(text_x, 'dp', axis=0, tiled=True)  300 us
    psum x1, waiting for transfers between devices, local(): summed = lax.psum(image_dx, 'mp')  42 us
  transfers between devices with their start and end apart: 5, of which 5 were waited for; matrix products, arithmetic and copies ran while one was open for 1% of the time, Pallas kernels for 0%

commit v1 on v0

v1 whole, which is shorter than its diff:
```python
import functools

import jax
import jax.numpy as jnp
from jax import lax
from jax.experimental import pallas as pl
from jax.experimental.pallas import tpu as pltpu
from jax.sharding import PartitionSpec as P

MESH = pl.DeviceIdType.MESH
F32, BF = jnp.float32, jnp.bfloat16
PIECE = 64
POS = {4: 0, 0: 1, 3: 2, 5: 3, 2: 4, 6: 5, 1: 6, 7: 7}


def dot(a, b):
    return jnp.dot(a, b, preferred_element_type=F32)


def dot_nt(a, b):
    return lax.dot_general(a, b, (((1,), (1,)), ((), ())), preferred_element_type=F32)


def dot_tn(a, b):
    return lax.dot_general(a, b, (((0,), (0,)), ((), ())), preferred_element_type=F32)


def kernel(total, fi_hbm, ft_hbm, wi_hbm, wt_hbm, lt_ref, bs_ref, oi_ref, ot_ref,
           feats, wts, featst, es, er, unit, scal, img, txt, dacc, prob, gi, gt,
           gib, r4a, r3a, r2a, r1a, r4b, r3b, r2b, r1b, sa, sb,
           sibr, gtb, tp4, tpr, tmr, zs, zr, fin, fst, fr, fx, ys, yr,
           lsem, ssem, rsem):
    dp, mp = lax.axis_index("dp"), lax.axis_index("mp")
    z, xl, y = dp // 8, (dp // 4) % 2, dp % 4
    c = mp % 2
    x = (mp // 2) * 2 + xl

    def dev(xx, yy, zz, cc):
        return (zz * 8 + (xx % 2) * 4 + yy, (xx // 2) * 2 + cc)

    xp, xm = dev((x + 1) % 4, y, z, c), dev((x + 3) % 4, y, z, c)
    yp, ym = dev(x, (y + 1) % 4, z, c), dev(x, (y + 3) % 4, z, c)
    zp, zm = dev(x, y, (z + 1) % 8, c), dev(x, y, (z + 7) % 8, c)
    y2 = dev(x, (y + 2) % 4, z, c)
    xo = (z * 8 + (1 - xl) * 4 + y, mp)
    sib = (dp, (mp // 2) * 2 + (1 - c))
    mps = [(dp, (mp + k) % 4) for k in (1, 2, 3)]

    barrier = pltpu.get_barrier_semaphore()
    greeted = mps + [xp, xm, yp, ym, zp, zm, y2]
    for d in greeted:
        pl.semaphore_signal(barrier, inc=1, device_id=d, device_id_type=MESH)

    loads = []
    for k, (s, t) in enumerate(((fi_hbm, feats.at[0, 0:224]), (wi_hbm, wts.at[0]),
                                (ft_hbm, feats.at[1, 0:224]), (wt_hbm, wts.at[1]))):
        cp = pltpu.make_async_copy(s, t, lsem.at[k])
        cp.start()
        loads.append(cp)
    feats[:, 224:256, :] = jnp.zeros((2, 32, 1152), BF)

    started = []

    def send(src, dst, to):
        k = len(started)
        cp = pltpu.make_async_remote_copy(src_ref=src, dst_ref=dst, send_sem=ssem.at[k],
                                          recv_sem=rsem.at[k], device_id=to, device_id_type=MESH)
        cp.start()
        started.append(cp)
        return cp

    place = (lax.broadcasted_iota(jnp.int32, (32, 128), 1)
             == lax.broadcasted_iota(jnp.int32, (32, 128), 0) + 32 * mp).astype(F32).astype(BF)
    emb_in = [[], []]
    for m in (0, 1):
        loads[2 * m].wait()
        loads[2 * m + 1].wait()
        main = dot(feats[m], wts[m, :, 0:256]).astype(BF)
        rest = dot(feats[m], wts[m, :, 256:288]).astype(BF)
        rest = dot(rest, place).astype(BF)
        for q in range(4):
            es[m, q, :, 0:256] = main[64 * q:64 * q + 64]
            es[m, q, :, 256:384] = rest[64 * q:64 * q + 64]
        if m == 0:
            pl.semaphore_wait(barrier, len(greeted))
        for k in (1, 2, 3):
            emb_in[m].append(send(es.at[m, (mp + k) % 4], er.at[m, mp], mps[k - 1]))
        er[m, mp] = es[m, mp]

    def normalize(m):
        for cp in emb_in[m]:
            cp.wait_recv()
        rest = sum(er[m, q, :, 256:384].astype(F32) for q in range(4))
        wide = jnp.concatenate([er[m, q, :, 0:256].astype(F32) for q in range(4)] + [rest], axis=1)
        scale = lax.rsqrt(jnp.sum(wide * wide, axis=1, keepdims=True) + 1e-06)
        unit[m] = wide * scale
        scal[m] = jnp.broadcast_to(scale, (64, 128))
        return (wide * scale).astype(BF)

    A, B = pl.ds(0, 32), pl.ds(32, 32)
    A0, A1, B0, B1 = pl.ds(0, 16), pl.ds(16, 16), pl.ds(32, 16), pl.ds(48, 16)
    got = {}
    img[0, 0] = normalize(0)
    got["A03"] = send(img.at[0, 0, A], img.at[0, 3, A], xp)
    got["A01"] = send(img.at[0, 0, A], img.at[0, 1, A], xm)
    got["B30"] = send(img.at[0, 0, B], img.at[3, 0, B], yp)
    got["B10"] = send(img.at[0, 0, B], img.at[1, 0, B], ym)
    got["A30"] = send(img.at[0, 0, A], img.at[3, 0, A], yp)
    got["A10"] = send(img.at[0, 0, A], img.at[1, 0, A], ym)
    got["B03"] = send(img.at[0, 0, B], img.at[0, 3, B], xp)
    got["B01"] = send(img.at[0, 0, B], img.at[0, 1, B], xm)

    txt[POS[0], 0] = normalize(1)
    tgot = {}
    sgot = []
    tgot[7] = send(txt.at[POS[0], 0], txt.at[POS[7], 0], zp)
    tgot[1] = send(txt.at[POS[0], 0], txt.at[POS[1], 0], zm)
    sgot.append(send(txt.at[POS[0], 0], txt.at[POS[0], 1], sib))

    def text_hop(k):
        for src, nxt, to, half in ((8 - k, 7 - k, zp, A), (k, k + 1, zm, B)):
            tgot[src].wait_recv()
            if k < 3:
                tgot[nxt] = send(txt.at[POS[src], 0], txt.at[POS[nxt], 0], to)
            else:
                tgot[(4, src)] = send(txt.at[POS[src], 0, half], txt.at[POS[4], 0, half], to)
            sgot.append(send(txt.at[POS[src], 0], txt.at[POS[src], 1], sib))

    got["A03"].wait_recv()
    got["A02+"] = send(img.at[0, 3, A0], img.at[0, 2, A0], xp)
    got["A01"].wait_recv()
    got["A02-"] = send(img.at[0, 1, A1], img.at[0, 2, A1], xm)
    got["B30"].wait_recv()
    got["B20+"] = send(img.at[3, 0, B0], img.at[2, 0, B0], yp)
    got["B10"].wait_recv()
    got["B20-"] = send(img.at[1, 0, B1], img.at[2, 0, B1], ym)

    def second(d):
        got["A3%d" % d] = send(img.at[0, d, A], img.at[3, d, A], yp)
        got["A1%d" % d] = send(img.at[0, d, A], img.at[1, d, A], ym)
        got["B%d3" % d] = send(img.at[d, 0, B], img.at[d, 3, B], xp)
        got["B%d1" % d] = send(img.at[d, 0, B], img.at[d, 1, B], xm)

    def third(d):
        got["A3%d" % d].wait_recv()
        got["A2%d+" % d] = send(img.at[3, d, A0], img.at[2, d, A0], yp)
        got["A1%d" % d].wait_recv()
        got["A2%d-" % d] = send(img.at[1, d, A1], img.at[2, d, A1], ym)
        got["B%d3" % d].wait_recv()
        got["B%d2+" % d] = send(img.at[d, 3, B0], img.at[d, 2, B0], xp)
        got["B%d1" % d].wait_recv()
        got["B%d2-" % d] = send(img.at[d, 1, B1], img.at[d, 2, B1], xm)

    second(1)
    second(3)
    text_hop(1)
    for k in ("A02+", "A02-", "B20+", "B20-"):
        got[k].wait_recv()
    second(2)
    third(0)
    text_hop(2)
    third(1)
    text_hop(3)
    third(3)
    tgot[(4, 5)].wait_recv()
    tgot[(4, 3)].wait_recv()
    sgot.append(send(txt.at[POS[4], 0], txt.at[POS[4], 1], sib))
    third(2)
    for m in (0, 1):
        for k in range(8):
            featst[m, k] = jnp.transpose(feats[m])[144 * k:144 * k + 144]
    for cp in sgot:
        cp.wait_recv()
    for d in range(4):
        for s in ("A2%d+", "A2%d-", "B%d2+", "B%d2-"):
            got[s % d].wait_recv()

    temp = jnp.exp(jnp.full((1, 1), lt_ref[0], F32))
    shift = jnp.full((1, 1), bs_ref[0], F32)
    gain = temp * (1.0 / total)
    text_all = txt[...].reshape(1024, 1152)

    def pairs(dy):
        dacc[...] = dot_nt(img[dy].reshape(256, 1152), text_all)

        def rows(i, _):
            at = pl.ds(pl.multiple_of(i * 16, 16), 16)
            logits = temp * dacc[at, :] + shift
            prob[pl.ds(pl.multiple_of(dy * 256 + i * 16, 16), 16), :] = (
                gain / (1.0 + jnp.exp(-logits))).astype(BF)
            return 0
        lax.fori_loop(0, 16, rows, 0, unroll=2)
        if dy == 0:
            logits = temp * dacc[0:64, 128:256] + shift
            same = (lax.broadcasted_iota(jnp.int32, (64, 128), 0)
                    == lax.broadcasted_iota(jnp.int32, (64, 128), 1))
            prob[0:64, 128:256] = jnp.where(
                same, -gain / (1.0 + jnp.exp(logits)), gain / (1.0 + jnp.exp(-logits))).astype(BF)
        gi[dy] = dot(prob[dy * 256:dy * 256 + 256, :], text_all).reshape(4, 64, 1152)

    pairs(2)
    gib[2, :, A] = gi[2, :, A].astype(BF)
    q4a = [send(gib.at[2, :, A0], r4a.at[:, A0], yp), send(gib.at[2, :, A1], r4a.at[:, A1], ym)]
    pairs(1)
    pairs(3)
    pairs(0)
    gib[:, 2, B] = gi[:, 2, B].astype(BF)
    q4b = [send(gib.at[:, 2, B0], r4b.at[:, A0], xp), send(gib.at[:, 2, B1], r4b.at[:, A1], xm)]

    def text_block(n):
        gt[2 * n:2 * n + 2] = dot_tn(prob[:, 256 * n:256 * n + 256],
                                     img[...].reshape(1024, 1152)).reshape(2, 2, 64, 1152)
        return send(gt.at[2 * n:2 * n + 2, 1], sibr.at[2 * n:2 * n + 2], sib)

    q0 = text_block(0)

    for cp in q4a:
        cp.wait_recv()
    for d in range(4):
        gib[1, d, A0] = (gi[1, d, A0] + r4a[d, A0].astype(F32)).astype(BF)
        gib[1, d, A1] = gi[1, d, A1].astype(BF)
        gib[3, d, A0] = gi[3, d, A0].astype(BF)
        gib[3, d, A1] = (gi[3, d, A1] + r4a[d, A1].astype(F32)).astype(BF)
    q3a = [send(gib.at[1, :, A], r3a.at[0], yp), send(gib.at[3, :, A], r3a.at[1], ym)]
    for cp in q4b:
        cp.wait_recv()
    for d in range(4):
        gib[d, 1, B0] = (gi[d, 1, B0] + r4b[d, A0].astype(F32)).astype(BF)
        gib[d, 1, B1] = gi[d, 1, B1].astype(BF)
        gib[d, 3, B0] = gi[d, 3, B0].astype(BF)
        gib[d, 3, B1] = (gi[d, 3, B1] + r4b[d, A1].astype(F32)).astype(BF)
    q3b = [send(gib.at[:, 1, B], r3b.at[0], xp), send(gib.at[:, 3, B], r3b.at[1], xm)]

    q0.wait_recv()
    gtb[POS[4]] = (gt[POS[4], 0] + sibr[POS[4]]).astype(BF)
    plus = send(gtb.at[POS[4], A], tp4.at[A], zp)
    minus = send(gtb.at[POS[4], B], tp4.at[B], zm)
    q1 = text_block(1)
    q2 = text_block(2)
    q3 = text_block(3)
    q1.wait_recv()
    plus.wait_recv()
    s3 = gt[POS[3], 0] + sibr[POS[3]]
    gtb[POS[3], A] = (s3[0:32] + tp4[A].astype(F32)).astype(BF)
    gtb[POS[3], B] = s3[32:64].astype(BF)
    plus = send(gtb.at[POS[3]], tpr.at[0], zp)
    minus.wait_recv()
    s3 = gt[POS[5], 0] + sibr[POS[5]]
    gtb[POS[5], A] = s3[0:32].astype(BF)
    gtb[POS[5], B] = (s3[32:64] + tp4[B].astype(F32)).astype(BF)
    minus = send(gtb.at[POS[5]], tmr.at[0], zm)
    for n, (a, b, q) in enumerate(((2, 6, q2), (1, 7, q3))):
        q.wait_recv()
        plus.wait_recv()
        gtb[POS[a]] = (gt[POS[a], 0] + sibr[POS[a]] + tpr[n].astype(F32)).astype(BF)
        plus = send(gtb.at[POS[a]], tpr.at[n + 1], zp)
        minus.wait_recv()
        gtb[POS[b]] = (gt[POS[b], 0] + sibr[POS[b]] + tmr[n].astype(F32)).astype(BF)
        minus = send(gtb.at[POS[b]], tmr.at[n + 1], zm)

    for cp in q3a:
        cp.wait_recv()
    for d in (2, 1, 3, 0):
        sa[d] = gi[0, d, A] + r3a[0, d].astype(F32) + r3a[1, d].astype(F32)
        if d == 2:
            q2a = [send(sa.at[2, A0], r2a.at[A0], xp), send(sa.at[2, A1], r2a.at[A1], xm)]
    for cp in q3b:
        cp.wait_recv()
    for d in (2, 1, 3, 0):
        sb[d] = gi[d, 0, B] + r3b[0, d].astype(F32) + r3b[1, d].astype(F32)
        if d == 2:
            q2b = [send(sb.at[2, A0], r2b.at[A0], yp), send(sb.at[2, A1], r2b.at[A1], ym)]
    last = []
    for q, s, r2, r1, fwd, back in ((q2a, sa, r2a, r1a, xp, xm), (q2b, sb, r2b, r1b, yp, ym)):
        for cp in q:
            cp.wait_recv()
        s[1, A0] += r2[A0]
        s[3, A1] += r2[A1]
        last.append(send(s.at[1], r1.at[0], fwd))
        last.append(send(s.at[3], r1.at[1], back))

    def back(m, dx):
        inner = jnp.sum(unit[m] * dx, axis=1, keepdims=True)
        dz = (scal[m][:, 0:1] * (dx - unit[m] * inner)).astype(BF)
        for q in range(4):
            zs[q, m, :, 0:256] = dz[:, 256 * q:256 * q + 256]
            zs[q, m, :, 256:384] = dz[:, 1024:1152]
        zr[mp, m] = zs[mp, m]
        return [send(zs.at[(mp + k) % 4, m], zr.at[mp, m], mps[k - 1]) for k in (1, 2, 3)]

    plus.wait_recv()
    minus.wait_recv()
    zin = back(1, gt[POS[0], 0] + sibr[POS[0]] + tpr[2].astype(F32) + tmr[2].astype(F32))
    for cp in last:
        cp.wait_recv()
    zin += back(0, jnp.concatenate([sa[0] + r1a[0] + r1a[1], sb[0] + r1b[0] + r1b[1]], axis=0))
    for cp in zin:
        cp.wait_recv()

    def gathered(m, cols):
        return jnp.concatenate([zr[q, m, :, cols] for q in range(4)], axis=0)

    i0 = lax.broadcasted_iota(jnp.int32, (128, 128), 0)
    i1 = lax.broadcasted_iota(jnp.int32, (128, 128), 1)
    pick_i = ((i0 == i1 + 32 * mp) & (i1 < 32)).astype(F32).astype(BF)
    pick_t = ((i0 == i1 - 32 + 32 * mp) & (i1 >= 32) & (i1 < 64)).astype(F32).astype(BF)
    zi, zt = gathered(0, slice(0, 256)), gathered(1, slice(0, 256))
    ri = dot(gathered(0, slice(256, 384)), pick_i).astype(BF)
    rt = dot(gathered(1, slice(256, 384)), pick_t).astype(BF)

    def chunk(dz):
        a, b = featst[0, (z + dz) % 8], featst[1, (z + dz) % 8]
        return jnp.concatenate([dot(a, zi), dot(b, zt), dot(a, ri) + dot(b, rt)], axis=1)

    H0, H1 = pl.ds(0, 80), pl.ds(80, 64)
    fst[4] = chunk(4).astype(BF)
    plus = send(fst.at[4, H0], fr.at[4, H0], zp)
    minus = send(fst.at[4, H1], fr.at[4, H1], zm)
    for a in (3, 2, 1):
        b = 8 - a
        fin[0] = chunk(a)
        fin[1] = chunk(b)
        plus.wait_recv()
        if a == 3:
            fin[0, H0] += fr[4, H0].astype(F32)
        else:
            fin[0] += fr[a + 1].astype(F32)
        fst[a] = fin[0].astype(BF)
        plus = send(fst.at[a], fr.at[a], zp)
        minus.wait_recv()
        if a == 3:
            fin[1, H1] += fr[4, H1].astype(F32)
        else:
            fin[1] += fr[b - 1].astype(F32)
        fst[b] = fin[1].astype(BF)
        minus = send(fst.at[b], fr.at[b], zm)
    fin[0] = chunk(0)
    plus.wait_recv()
    minus.wait_recv()
    summed = fin[0] + fr[1].astype(F32) + fr[7].astype(F32)
    fx[0] = summed[0:72]
    fx[1] = summed[72:144]
    cp = send(fx.at[1 - xl], fx.at[2], xo)
    cp.wait_recv()
    summed = fx[xl] + fx[2]
    for k in range(4):
        ys[k, 0:18] = summed[18 * k:18 * k + 18]
        ys[k, 18:24] = jnp.zeros((6, 640), F32)
    q = [send(ys.at[(y + 2) % 4], yr.at[1], y2), send(ys.at[(y + 1) % 4], yr.at[0], yp),
         send(ys.at[(y + 3) % 4], yr.at[2], ym)]
    for cp in q:
        cp.wait_recv()
    out = ys[y] + yr[0] + yr[1] + yr[2]
    oi_ref[:, 0:256] = out[0:18, 0:256]
    oi_ref[:, 256:288] = out[0:18, 512:544]
    ot_ref[:, 0:256] = out[0:18, 256:512]
    ot_ref[:, 256:288] = pltpu.roll(out[:, 512:640], 96, 1)[0:18, 0:32]
    for cp in started:
        cp.wait_send()


COPIES = 200


def local(image_feats, text_feats, image_proj, text_proj, log_temp, bias):
    total = image_feats.shape[0] * lax.axis_size("dp")
    vm = pltpu.VMEM
    out = jax.ShapeDtypeStruct((18, 288), F32)
    return pl.pallas_call(
        functools.partial(kernel, total),
        out_shape=(out, out),
        in_specs=[pl.BlockSpec(memory_space=pl.ANY)] * 4
        + [pl.BlockSpec(memory_space=pltpu.SMEM)] * 2,
        out_specs=(pl.BlockSpec(memory_space=vm), pl.BlockSpec(memory_space=vm)),
        scratch_shapes=[
            vm((2, 256, 1152), BF),
            vm((2, 1152, 288), BF),
            vm((2, 8, 144, 256), BF),
            vm((2, 4, 64, 384), BF),
            vm((2, 4, 64, 384), BF),
            vm((2, 64, 1152), F32),
            vm((2, 64, 128), F32),
            vm((4, 4, 64, 1152), BF),
            vm((8, 2, 64, 1152), BF),
            vm((256, 1024), F32),
            vm((1024, 1024), BF),
            vm((4, 4, 64, 1152), F32),
            vm((8, 2, 64, 1152), F32),
            vm((4, 4, 64, 1152), BF),
            vm((4, 32, 1152), BF),
            vm((2, 4, 32, 1152), BF),
            vm((32, 1152), F32),
            vm((2, 32, 1152), F32),
            vm((4, 32, 1152), BF),
            vm((2, 4, 32, 1152), BF),
            vm((32, 1152), F32),
            vm((2, 32, 1152), F32),
            vm((4, 32, 1152), F32),
            vm((4, 32, 1152), F32),
            vm((8, 64, 1152), F32),
            vm((8, 64, 1152), BF),
            vm((64, 1152), BF),
            vm((3, 64, 1152), BF),
            vm((3, 64, 1152), BF),
            vm((4, 2, 64, 384), BF),
            vm((4, 2, 64, 384), BF),
            vm((2, 144, 640), F32),
            vm((8, 144, 640), BF),
            vm((8, 144, 640), BF),
            vm((3, 72, 640), F32),
            vm((4, 24, 640), F32),
            vm((3, 24, 640), F32),
            pltpu.SemaphoreType.DMA((4,)),
            pltpu.SemaphoreType.DMA((COPIES,)),
            pltpu.SemaphoreType.DMA((COPIES,)),
        ],
        name="contrastive",
        compiler_params=pltpu.CompilerParams(
            collective_id=0, has_side_effects=True, vmem_limit_bytes=60 * 2**20
        ),
    )(image_feats, text_feats, image_proj, text_proj, log_temp, bias)


def solution(mesh):
    placed = (P("dp", None), P("dp", None), P(None, "mp"), P(None, "mp"), P(), P())
    return jax.shard_map(
        local, mesh=mesh, in_specs=placed, out_specs=(P("dp", "mp"), P("dp", "mp")), check_vma=False
    )
```

time: 1370 us -> 123 us (0.09)
  waiting for transfers between devices: 1290 us -> 0 us
  Pallas kernels: 0 us -> 113 us
  matrix products: 27.4 us -> 0 us
  blocking collectives: 18.6 us -> 0 us
  between operations: 15.9 us -> 1.95 us
    unnamed x6 -> x0, waiting for transfers between devices: 946 us -> none
    all_gather x1 -> x0, waiting for transfers between devices: 300 us -> none  [local(): piece = lax.all_gather(text_x, 'dp', axis=0, tiled=True)]
    pallas_call x0 -> x1, Pallas kernels: none -> 113 us  [local(): pl.pallas_call(functools.partial(kernel, total), out_shape=(out, out), in...]
    psum x1 -> x0, waiting for transfers between devices: 42 us -> none  [local(): summed = lax.psum(image_dx, 'mp')]
    dot_general x7 -> x0, matrix products: 27.4 us -> none  [the longest x3 13.6 us: contract_rows(): lax.dot_general(left, right, (((0,), (0,)), ((), ())), preferred_element_...]
  transfers between devices with their start and end apart: 5 -> 0, of which waited for: 5 -> 0; matrix products, arithmetic and copies ran while one was open for 1% -> 0% of each run, Pallas kernels for 0% -> 0%
where the time goes in v1:
time: 123 us; the launch traced here: 120 us
  Pallas kernels  113 us (92%)
  local copies, waits for them, and re-layouts  5.68 us (5%)
  between operations  1.95 us (2%)
    pallas_call x1, Pallas kernels, local(): pl.pallas_call(functools.partial(kernel, total), out_shape=(out, out), in...  113 us
    unnamed x8, local copies, waits for them, and re-layouts  5.68 us

profile of v1, /device:TPU:2, one launch (start us, length us, event | category | flops | bytes accessed | tf_op | source)
XLA Modules:
  0.0 120.2 jit_solution(1058265205303076274)
XLA Ops:
  1.9 0.0 copy-start
  1.9 2.4 %copy.8.wi_hbm = bf16[1152,288]{1,0:T(8,128)(2,1)} copy(bf16[1152,288]{0,1:T(8,128)(2,1)} %param.8) | data formatting | bytes 1327104 | tf_op args[2]
  4.3 0.0 copy-done
  4.3 1.3 %copy.9.wt_hbm = bf16[1152,288]{1,0:T(8,128)(2,1)} copy(bf16[1152,288]{0,1:T(8,128)(2,1)S(1)} %copy-done) | data formatting | bytes 1327104 | tf_op args[3]
  5.6 112.6 %contrastive.1 = (f32[18,288]{1,0:T(8,128)}, f32[18,288]{1,0:T(8,128)}) custom-call(bf16[224,1152]{1,0:T(8,128)(2,1)} %fi_hbm.1, bf16[224,1152]{1,0:T(8,128)(2,1)} %ft_hbm.1, bf16[1152,288]{1,0:T(8,128)(2,1)} %copy.8.wi_hbm, bf16[1152,288]{1,0:T(8,128)(2,1)} %copy.9.wt_hbm, f32[1]{0:T(128)S(6)} %copy.12.lt_ref, f32[1]{0:T(128)S(6)} %copy.13.bs_ref), custom_call_target="tpu_custom_call" | custom-call | tf_op jit(solution)/shard_map/contrastive/pallas_call | solution.py:369
  118.2 0.0 copy-start.1
  118.2 1.4 %copy.14 = f32[18,288]{1,0:T(8,128)} copy(f32[18,288]{1,0:T(8,128)} %get-tuple-element.4) | data formatting | bytes 41472
  119.6 0.0 copy-done.1
  119.6 0.6 copy.15
Async XLA Ops:
  1.9 2.4 %copy-start = (bf16[1152,288]{0,1:T(8,128)(2,1)S(1)}, bf16[1152,288]{0,1:T(8,128)(2,1)}, u32[]{:S(2)}) copy-start(bf16[1152,288]{0,1:T(8,128)(2,1)} %param.9) | copy-start | bytes 1990660
  118.2 1.4 %copy-start.1 = (f32[18,288]{1,0:T(8,128)S(1)}, f32[18,288]{1,0:T(8,128)}, u32[]{:S(2)}) copy-start(f32[18,288]{1,0:T(8,128)} %get-tuple-element.5) | copy-start | bytes 62212

commit v2 on v1

v2 whole, which is shorter than its diff:
```python
import functools

import jax
import jax.numpy as jnp
from jax import lax
from jax.experimental import pallas as pl
from jax.experimental.pallas import tpu as pltpu
from jax.sharding import PartitionSpec as P

MESH = pl.DeviceIdType.MESH
F32, BF = jnp.float32, jnp.bfloat16
PIECE = 64
POS = {4: 0, 0: 1, 3: 2, 5: 3, 2: 4, 6: 5, 1: 6, 7: 7}


def dot(a, b):
    return jnp.dot(a, b, preferred_element_type=F32)


def dot_nt(a, b):
    return lax.dot_general(a, b, (((1,), (1,)), ((), ())), preferred_element_type=F32)


def dot_tn(a, b):
    return lax.dot_general(a, b, (((0,), (0,)), ((), ())), preferred_element_type=F32)


def kernel(total, fi_hbm, ft_hbm, wi_hbm, wt_hbm, lt_ref, bs_ref, oi_ref, ot_ref,
           feats, wts, featst, es, er, unit, scal, img, txt, prob, gi, gt,
           gib, ra, rb, ra2, rb2, sa, sb, sab, sbb,
           sibr, gtb, tp4, tpr, tmr, zs, zr, fst, fr, ys, yr,
           lsem, ssem, rsem):
    dp, mp = lax.axis_index("dp"), lax.axis_index("mp")
    z, xl, y = dp // 8, (dp // 4) % 2, dp % 4
    c = mp % 2
    x = (mp // 2) * 2 + xl

    def dev(xx, yy, zz, cc):
        return (zz * 8 + (xx % 2) * 4 + yy, (xx // 2) * 2 + cc)

    xp, x2, xm = (dev((x + k) % 4, y, z, c) for k in (1, 2, 3))
    yp, y2, ym = (dev(x, (y + k) % 4, z, c) for k in (1, 2, 3))
    zs_at = [dev(x, y, (z + k) % 8, c) for k in range(8)]
    zp, zm = zs_at[1], zs_at[7]
    ws_at = [(z * 8 + ((xl + k // 4) % 2) * 4 + (y + k) % 4, mp) for k in range(8)]
    sib = (dp, (mp // 2) * 2 + (1 - c))
    mps = [(dp, (mp + k) % 4) for k in (1, 2, 3)]

    barrier = pltpu.get_barrier_semaphore()
    greeted = mps + [xp, xm] + zs_at[1:] + ws_at[1:4] + ws_at[5:]
    for d in greeted:
        pl.semaphore_signal(barrier, inc=1, device_id=d, device_id_type=MESH)

    loads = []
    for k, (s, t) in enumerate(((fi_hbm, feats.at[0, 0:224]), (wi_hbm, wts.at[0]),
                                (ft_hbm, feats.at[1, 0:224]), (wt_hbm, wts.at[1]))):
        cp = pltpu.make_async_copy(s, t, lsem.at[k])
        cp.start()
        loads.append(cp)
    feats[:, 224:256, :] = jnp.zeros((2, 32, 1152), BF)

    started = []

    def send(src, dst, to):
        k = len(started)
        cp = pltpu.make_async_remote_copy(src_ref=src, dst_ref=dst, send_sem=ssem.at[k],
                                          recv_sem=rsem.at[k], device_id=to, device_id_type=MESH)
        cp.start()
        started.append(cp)
        return cp

    place = (lax.broadcasted_iota(jnp.int32, (32, 128), 1)
             == lax.broadcasted_iota(jnp.int32, (32, 128), 0) + 32 * mp).astype(F32).astype(BF)
    emb_in = [[], []]
    for m in (0, 1):
        loads[2 * m].wait()
        loads[2 * m + 1].wait()
        main = dot_nt(feats[m], wts[m, 0:256, :]).astype(BF)
        rest = dot_nt(feats[m], wts[m, 256:288, :]).astype(BF)
        rest = dot(rest, place).astype(BF)
        for q in range(4):
            es[m, q, :, 0:256] = main[64 * q:64 * q + 64]
            es[m, q, :, 256:384] = rest[64 * q:64 * q + 64]
        if m == 0:
            pl.semaphore_wait(barrier, len(greeted))
        for k in (1, 2, 3):
            emb_in[m].append(send(es.at[m, (mp + k) % 4], er.at[m, mp], mps[k - 1]))
        er[m, mp] = es[m, mp]

    def normalize(m):
        for cp in emb_in[m]:
            cp.wait_recv()
        rest = sum(er[m, q, :, 256:384].astype(F32) for q in range(4))
        wide = jnp.concatenate([er[m, q, :, 0:256].astype(F32) for q in range(4)] + [rest], axis=1)
        scale = lax.rsqrt(jnp.sum(wide * wide, axis=1, keepdims=True) + 1e-06)
        unit[m] = wide * scale
        scal[m] = jnp.broadcast_to(scale, (64, 128))
        return (wide * scale).astype(BF)

    A, B = pl.ds(0, 32), pl.ds(32, 32)
    A0, A1, B0, B1 = pl.ds(0, 16), pl.ds(16, 16), pl.ds(32, 16), pl.ds(48, 16)
    got = {}
    img[0, 0] = normalize(0)
    got["A03"] = send(img.at[0, 0, A], img.at[0, 3, A], xp)
    got["A01"] = send(img.at[0, 0, A], img.at[0, 1, A], xm)
    got["B30"] = send(img.at[0, 0, B], img.at[3, 0, B], yp)
    got["B10"] = send(img.at[0, 0, B], img.at[1, 0, B], ym)
    got["A02"] = send(img.at[0, 0, A], img.at[0, 2, A], x2)
    got["B20"] = send(img.at[0, 0, B], img.at[2, 0, B], y2)
    got["A30"] = send(img.at[0, 0, A], img.at[3, 0, A], yp)
    got["A10"] = send(img.at[0, 0, A], img.at[1, 0, A], ym)
    got["B03"] = send(img.at[0, 0, B], img.at[0, 3, B], xp)
    got["B01"] = send(img.at[0, 0, B], img.at[0, 1, B], xm)

    txt[POS[0], 0] = normalize(1)
    tgot = {}
    sgot = []
    tgot[7] = send(txt.at[POS[0], 0], txt.at[POS[7], 0], zp)
    tgot[1] = send(txt.at[POS[0], 0], txt.at[POS[1], 0], zm)
    sgot.append(send(txt.at[POS[0], 0], txt.at[POS[0], 1], sib))

    def text_hop(k):
        for src, nxt, to, half in ((8 - k, 7 - k, zp, A), (k, k + 1, zm, B)):
            tgot[src].wait_recv()
            if k < 3:
                tgot[nxt] = send(txt.at[POS[src], 0], txt.at[POS[nxt], 0], to)
            else:
                tgot[(4, src)] = send(txt.at[POS[src], 0, half], txt.at[POS[4], 0, half], to)
            sgot.append(send(txt.at[POS[src], 0], txt.at[POS[src], 1], sib))

    wide_t = jnp.transpose(feats[0])
    for k in range(8):
        featst[0, k] = wide_t[144 * k:144 * k + 144]
    p0 = lax.broadcasted_iota(jnp.int32, (144, 1152), 0)
    at_z = p0 + 126 * ((p0 * 3641) >> 16)
    p1 = lax.broadcasted_iota(jnp.int32, (144, 1152), 1)

    def turn(w, _):
        featst[1, w] = dot_nt((p1 == at_z + 18 * w).astype(F32).astype(BF), feats[1]).astype(BF)
        return 0
    lax.fori_loop(0, 8, turn, 0)

    def second(d):
        got["A3%d" % d] = send(img.at[0, d, A], img.at[3, d, A], yp)
        got["A1%d" % d] = send(img.at[0, d, A], img.at[1, d, A], ym)
        got["B%d3" % d] = send(img.at[d, 0, B], img.at[d, 3, B], xp)
        got["B%d1" % d] = send(img.at[d, 0, B], img.at[d, 1, B], xm)

    def third(d):
        got["A3%d" % d].wait_recv()
        got["A2%d+" % d] = send(img.at[3, d, A0], img.at[2, d, A0], yp)
        got["A1%d" % d].wait_recv()
        got["A2%d-" % d] = send(img.at[1, d, A1], img.at[2, d, A1], ym)
        got["B%d3" % d].wait_recv()
        got["B%d2+" % d] = send(img.at[d, 3, B0], img.at[d, 2, B0], xp)
        got["B%d1" % d].wait_recv()
        got["B%d2-" % d] = send(img.at[d, 1, B1], img.at[d, 2, B1], xm)

    for k in ("A03", "A01", "B30", "B10"):
        got[k].wait_recv()
    second(1)
    second(3)
    text_hop(1)
    for k in ("A02", "B20"):
        got[k].wait_recv()
    second(2)
    third(0)
    text_hop(2)
    third(1)
    third(3)
    text_hop(3)
    third(2)

    temp = jnp.exp(jnp.full((1, 1), lt_ref[0], F32))
    shift = jnp.full((1, 1), bs_ref[0], F32)
    gain = temp * (1.0 / total)

    def scores(dy, n):
        at = pl.ds(2 * n, 2)
        logits = temp * dot_nt(img[dy].reshape(256, 1152), txt[at].reshape(256, 1152)) + shift
        cols = pl.ds(pl.multiple_of(256 * n, 256), 256)
        prob[256 * dy:256 * dy + 256, cols] = (gain / (1.0 + jnp.exp(-logits))).astype(BF)
        return logits

    def early(dy):
        for d in range(4) if dy == 2 else ():
            got["A2%d+" % d].wait_recv()
            got["A2%d-" % d].wait_recv()
        got["B%d2+" % dy].wait_recv()
        got["B%d2-" % dy].wait_recv()

        def some(i, _):
            scores(dy, 3 - i)
            return 0
        lax.fori_loop(0, 3, some, 0)

    def late(dy):
        logits = scores(dy, 0)
        if dy == 0:
            logits = logits[0:64, 128:256]
            same = (lax.broadcasted_iota(jnp.int32, (64, 128), 0)
                    == lax.broadcasted_iota(jnp.int32, (64, 128), 1))
            prob[0:64, 128:256] = jnp.where(
                same, -gain / (1.0 + jnp.exp(logits)), gain / (1.0 + jnp.exp(-logits))).astype(BF)
        gi[dy] = dot(prob[256 * dy:256 * dy + 256, :],
                     txt[...].reshape(1024, 1152)).reshape(4, 64, 1152)
        gib[dy] = gi[dy].astype(BF)
        if dy:
            qa.append(send(gib.at[dy, :, A], ra.at[dy - 1], (yp, y2, ym)[dy - 1]))
        for d in (2, 1, 3):
            qb.append(send(gib.at[dy, d, B], rb.at[d - 1, dy], (xp, x2, xm)[d - 1]))

    qa, qb = [], []
    for cp in sgot:
        cp.wait_recv()
    early(0)
    tgot[(4, 5)].wait_recv()
    tgot[(4, 3)].wait_recv()
    last_sib = send(txt.at[POS[4], 0], txt.at[POS[4], 1], sib)
    early(1)
    early(3)
    last_sib.wait_recv()
    late(1)
    late(3)
    late(0)
    early(2)
    late(2)

    def text_block(n):
        gt[2 * n:2 * n + 2] = dot_tn(prob[:, 256 * n:256 * n + 256],
                                     img[...].reshape(1024, 1152)).reshape(2, 2, 64, 1152)
        return send(gt.at[2 * n:2 * n + 2, 1], sibr.at[2 * n:2 * n + 2], sib)

    q0 = text_block(0)
    q1 = text_block(1)
    q0.wait_recv()
    gtb[POS[4]] = (gt[POS[4], 0] + sibr[POS[4]]).astype(BF)
    plus = send(gtb.at[POS[4], A], tp4.at[A], zp)
    minus = send(gtb.at[POS[4], B], tp4.at[B], zm)
    q2 = text_block(2)
    q3 = text_block(3)
    q1.wait_recv()
    plus.wait_recv()
    s3 = gt[POS[3], 0] + sibr[POS[3]]
    gtb[POS[3], A] = (s3[0:32] + tp4[A].astype(F32)).astype(BF)
    gtb[POS[3], B] = s3[32:64].astype(BF)
    plus = send(gtb.at[POS[3]], tpr.at[0], zp)
    minus.wait_recv()
    s3 = gt[POS[5], 0] + sibr[POS[5]]
    gtb[POS[5], A] = s3[0:32].astype(BF)
    gtb[POS[5], B] = (s3[32:64] + tp4[B].astype(F32)).astype(BF)
    minus = send(gtb.at[POS[5]], tmr.at[0], zm)
    for n, (a, b, q) in enumerate(((2, 6, q2), (1, 7, q3))):
        q.wait_recv()
        plus.wait_recv()
        gtb[POS[a]] = (gt[POS[a], 0] + sibr[POS[a]] + tpr[n].astype(F32)).astype(BF)
        plus = send(gtb.at[POS[a]], tpr.at[n + 1], zp)
        minus.wait_recv()
        gtb[POS[b]] = (gt[POS[b], 0] + sibr[POS[b]] + tmr[n].astype(F32)).astype(BF)
        minus = send(gtb.at[POS[b]], tmr.at[n + 1], zm)

    for cp in qa:
        cp.wait_recv()
    qa2, qb2 = [], []
    for d in (2, 1, 3, 0):
        sa[d] = gi[0, d, A] + ra[0, d].astype(F32) + ra[1, d].astype(F32) + ra[2, d].astype(F32)
        if d:
            sab[d - 1] = sa[d].astype(BF)
            qa2.append(send(sab.at[d - 1], ra2.at[d - 1], (xp, x2, xm)[d - 1]))
    for cp in qb:
        cp.wait_recv()
    for d in (2, 1, 3, 0):
        sb[d] = gi[d, 0, B] + rb[0, d].astype(F32) + rb[1, d].astype(F32) + rb[2, d].astype(F32)
        if d:
            sbb[d - 1] = sb[d].astype(BF)
            qb2.append(send(sbb.at[d - 1], rb2.at[d - 1], (yp, y2, ym)[d - 1]))

    def back(m, dx):
        inner = jnp.sum(unit[m] * dx, axis=1, keepdims=True)
        dz = (scal[m][:, 0:1] * (dx - unit[m] * inner)).astype(BF)
        for q in range(4):
            zs[m, q, :, 0:256] = dz[:, 256 * q:256 * q + 256]
            zs[m, q, :, 256:384] = dz[:, 1024:1152]
        zr[m, mp] = zs[m, mp]
        return [send(zs.at[m, (mp + k) % 4], zr.at[m, mp], mps[k - 1]) for k in (1, 2, 3)]

    plus.wait_recv()
    minus.wait_recv()
    zt_in = back(1, gt[POS[0], 0] + sibr[POS[0]] + tpr[2].astype(F32) + tmr[2].astype(F32))
    for cp in qa2 + qb2:
        cp.wait_recv()
    sums = [s[0] + r[0].astype(F32) + r[1].astype(F32) + r[2].astype(F32)
            for s, r in ((sa, ra2), (sb, rb2))]
    zi_in = back(0, jnp.concatenate(sums, axis=0))

    pick = (lax.broadcasted_iota(jnp.int32, (128, 128), 0)
            == lax.broadcasted_iota(jnp.int32, (128, 128), 1) + 32 * mp)
    pick = (pick & (lax.broadcasted_iota(jnp.int32, (128, 128), 1) < 32)).astype(F32).astype(BF)
    far_z, far_w = (4, 3, 5, 2, 6, 1, 7), (6, 2, 5, 7, 1, 3, 4)

    def first(m, arrived, far, base, at):
        for cp in arrived:
            cp.wait_recv()
        rest = jnp.concatenate([zr[m, q, :, 256:384] for q in range(4)], axis=0)
        grads = jnp.concatenate(
            [jnp.concatenate([zr[m, q, :, 0:256] for q in range(4)], axis=0),
             dot(rest, pick).astype(BF)], axis=1)
        q = []
        for k in far:
            fst[m, k] = dot(featst[m, base(k)], grads).astype(BF)
            q.append(send(fst.at[m, k], fr.at[m, k], at[k]))
        return q, dot(featst[m, base(0)], grads)

    def second_sum(m, q, own, far, base, at):
        for cp in q:
            cp.wait_recv()
        summed = own
        for k in far:
            summed = summed + fr[m, k].astype(F32)
        for k in range(8):
            ys[m, k, 0:18] = summed[18 * k:18 * k + 18]
            ys[m, k, 18:24] = jnp.zeros((6, 384), F32)
        return [send(ys.at[m, base(k)], yr.at[m, k], at[k]) for k in far]

    def by_z(k):
        return (z + k) % 8

    def by_w(k):
        return ((xl + k // 4) % 2) * 4 + (y + k) % 4

    qt, own_t = first(1, zt_in, far_w, by_w, ws_at)
    qi, own_i = first(0, zi_in, far_z, by_z, zs_at)
    qt2 = second_sum(1, qt, own_t, far_z, by_z, zs_at)
    qi2 = second_sum(0, qi, own_i, far_w, by_w, ws_at)
    for m, q, base, ref in ((1, qt2, by_z, ot_ref), (0, qi2, by_w, oi_ref)):
        for cp in q:
            cp.wait_recv()
        out = ys[m, base(0)]
        for k in range(1, 8):
            out = out + yr[m, k]
        ref[...] = out[0:18, 0:288]
    for cp in started:
        cp.wait_send()


COPIES = 256


def local(image_feats, text_feats, image_proj, text_proj, log_temp, bias):
    total = image_feats.shape[0] * lax.axis_size("dp")
    vm = pltpu.VMEM
    out = jax.ShapeDtypeStruct((18, 288), F32)
    return pl.pallas_call(
        functools.partial(kernel, total),
        out_shape=(out, out),
        in_specs=[pl.BlockSpec(memory_space=pl.ANY)] * 4
        + [pl.BlockSpec(memory_space=pltpu.SMEM)] * 2,
        out_specs=(pl.BlockSpec(memory_space=vm), pl.BlockSpec(memory_space=vm)),
        scratch_shapes=[
            vm((2, 256, 1152), BF),
            vm((2, 288, 1152), BF),
            vm((2, 8, 144, 256), BF),
            vm((2, 4, 64, 384), BF),
            vm((2, 4, 64, 384), BF),
            vm((2, 64, 1152), F32),
            vm((2, 64, 128), F32),
            vm((4, 4, 64, 1152), BF),
            vm((8, 2, 64, 1152), BF),
            vm((1024, 1024), BF),
            vm((4, 4, 64, 1152), F32),
            vm((8, 2, 64, 1152), F32),
            vm((4, 4, 64, 1152), BF),
            vm((3, 4, 32, 1152), BF),
            vm((3, 4, 32, 1152), BF),
            vm((3, 32, 1152), BF),
            vm((3, 32, 1152), BF),
            vm((4, 32, 1152), F32),
            vm((4, 32, 1152), F32),
            vm((3, 32, 1152), BF),
            vm((3, 32, 1152), BF),
            vm((8, 64, 1152), F32),
            vm((8, 64, 1152), BF),
            vm((64, 1152), BF),
            vm((3, 64, 1152), BF),
            vm((3, 64, 1152), BF),
            vm((2, 4, 64, 384), BF),
            vm((2, 4, 64, 384), BF),
            vm((2, 8, 144, 384), BF),
            vm((2, 8, 144, 384), BF),
            vm((2, 8, 24, 384), F32),
            vm((2, 8, 24, 384), F32),
            pltpu.SemaphoreType.DMA((4,)),
            pltpu.SemaphoreType.DMA((COPIES,)),
            pltpu.SemaphoreType.DMA((COPIES,)),
        ],
        name="contrastive",
        compiler_params=pltpu.CompilerParams(
            collective_id=0, has_side_effects=True, vmem_limit_bytes=60 * 2**20
        ),
    )(image_feats, text_feats, image_proj.T, text_proj.T, log_temp, bias)


def solution(mesh):
    placed = (P("dp", None), P("dp", None), P(None, "mp"), P(None, "mp"), P(), P())
    return jax.shard_map(
        local, mesh=mesh, in_specs=placed, out_specs=(P("dp", "mp"), P("dp", "mp")), check_vma=False
    )
```

time: 123 us -> 111 us (0.902)
  Pallas kernels: 113 us -> 105 us
  local copies, waits for them, and re-layouts: 5.68 us -> 2.01 us
    pallas_call x1, Pallas kernels: 113 us -> 105 us  [local(): pl.pallas_call(functools.partial(kernel, total), out_shape=(out, out), in...]
    unnamed x8 -> x4, local copies, waits for them, and re-layouts: 5.68 us -> 2.01 us
where the time goes in v2:
time: 111 us; the launch traced here: 109 us
  Pallas kernels  105 us (95%)
  local copies, waits for them, and re-layouts  2.01 us (2%)
  between operations  1.94 us (2%)
    pallas_call x1, Pallas kernels, local(): pl.pallas_call(functools.partial(kernel, total), out_shape=(out, out), in...  105 us

profile of v2, /device:TPU:2, one launch (start us, length us, event | category | flops | bytes accessed | tf_op | source)
XLA Modules:
  0.0 109.3 jit_solution(9956738747142022903)
XLA Ops:
  1.9 105.4 %contrastive.1 = (f32[18,288]{1,0:T(8,128)}, f32[18,288]{1,0:T(8,128)}) custom-call(bf16[224,1152]{1,0:T(8,128)(2,1)} %fi_hbm.1, bf16[224,1152]{1,0:T(8,128)(2,1)} %ft_hbm.1, bf16[288,1152]{1,0:T(8,128)(2,1)} %bitcast.2, bf16[288,1152]{1,0:T(8,128)(2,1)} %bitcast.3, f32[1]{0:T(128)S(6)} %copy.10.lt_ref, f32[1]{0:T(128)S(6)} %copy.11.bs_ref), custom_call_target="tpu_custom_call" | custom-call | tf_op jit(solution)/shard_map/contrastive/pallas_call | solution.py:353
  107.3 0.0 copy-start
  107.3 1.4 %copy.12 = f32[18,288]{1,0:T(8,128)} copy(f32[18,288]{1,0:T(8,128)} %get-tuple-element.4) | data formatting | bytes 41472
  108.7 0.0 copy-done
  108.7 0.6 copy.13
Async XLA Ops:
  107.3 1.4 %copy-start = (f32[18,288]{1,0:T(8,128)S(1)}, f32[18,288]{1,0:T(8,128)}, u32[]{:S(2)}) copy-start(f32[18,288]{1,0:T(8,128)} %get-tuple-element.5) | copy-start | bytes 62212

commit v3 on v2

v3 whole, which is shorter than its diff:
```python
import functools

import jax
import jax.numpy as jnp
from jax import lax
from jax.experimental import pallas as pl
from jax.experimental.pallas import tpu as pltpu
from jax.sharding import PartitionSpec as P

MESH = pl.DeviceIdType.MESH
F32, BF = jnp.float32, jnp.bfloat16
PIECE = 64
POS = {4: 0, 0: 1, 3: 2, 5: 3, 2: 4, 6: 5, 1: 6, 7: 7}


def dot(a, b):
    return jnp.dot(a, b, preferred_element_type=F32)


def dot_nt(a, b):
    return lax.dot_general(a, b, (((1,), (1,)), ((), ())), preferred_element_type=F32)


def dot_tn(a, b):
    return lax.dot_general(a, b, (((0,), (0,)), ((), ())), preferred_element_type=F32)


def kernel(total, fi_hbm, ft_hbm, wi_hbm, wt_hbm, lt_ref, bs_ref, oi_ref, ot_ref,
           feats, wts, featst, es, er, unit, scal, img, txt, prob, gi, gt,
           gib, ra, ra2, sa, sab, sibr, gtb, tp4, tpr, tmr, zs, zr,
           fsi, fri, fst, frt, ysi, yri, yst, yrt,
           lsem, ssem, rsem):
    dp, mp = lax.axis_index("dp"), lax.axis_index("mp")
    z, xl, y = dp // 8, (dp // 4) % 2, dp % 4
    c = mp % 2
    x = (mp // 2) * 2 + xl

    def dev(xx, yy, zz, cc):
        return (zz * 8 + (xx % 2) * 4 + yy, (xx // 2) * 2 + cc)

    xp, x2, xm = (dev((x + k) % 4, y, z, c) for k in (1, 2, 3))
    yp, y2, ym = (dev(x, (y + k) % 4, z, c) for k in (1, 2, 3))
    zs_at = [dev(x, y, (z + k) % 8, c) for k in range(8)]
    zp, zm = zs_at[1], zs_at[7]
    ws_at = [(z * 8 + ((xl + k // 4) % 2) * 4 + (y + k) % 4, mp) for k in range(8)]
    sib = (dp, (mp // 2) * 2 + (1 - c))
    mps = [(dp, (mp + k) % 4) for k in (1, 2, 3)]

    barrier = pltpu.get_barrier_semaphore()
    greeted = mps + [xp, xm] + zs_at[1:] + ws_at[1:4] + ws_at[5:]
    for d in greeted:
        pl.semaphore_signal(barrier, inc=1, device_id=d, device_id_type=MESH)

    loads = []
    for k, (s, t) in enumerate(((fi_hbm, feats.at[0, 0:224]), (wi_hbm, wts.at[0]),
                                (ft_hbm, feats.at[1, 0:224]), (wt_hbm, wts.at[1]))):
        cp = pltpu.make_async_copy(s, t, lsem.at[k])
        cp.start()
        loads.append(cp)
    feats[:, 224:256, :] = jnp.zeros((2, 32, 1152), BF)

    started = []

    def send(src, dst, to):
        k = len(started)
        cp = pltpu.make_async_remote_copy(src_ref=src, dst_ref=dst, send_sem=ssem.at[k],
                                          recv_sem=rsem.at[k], device_id=to, device_id_type=MESH)
        cp.start()
        started.append(cp)
        return cp

    place = (lax.broadcasted_iota(jnp.int32, (32, 128), 1)
             == lax.broadcasted_iota(jnp.int32, (32, 128), 0) + 32 * mp).astype(F32).astype(BF)
    emb_in = [[], []]
    for m in (0, 1):
        loads[2 * m].wait()
        loads[2 * m + 1].wait()
        main = dot_nt(feats[m], wts[m, 0:256, :]).astype(BF)
        rest = dot_nt(feats[m], wts[m, 256:288, :]).astype(BF)
        rest = dot(rest, place).astype(BF)
        for q in range(4):
            es[m, q, :, 0:256] = main[64 * q:64 * q + 64]
            es[m, q, :, 256:384] = rest[64 * q:64 * q + 64]
        if m == 0:
            pl.semaphore_wait(barrier, len(greeted))
        for k in (1, 2, 3):
            emb_in[m].append(send(es.at[m, (mp + k) % 4], er.at[m, mp], mps[k - 1]))
        er[m, mp] = es[m, mp]

    def normalize(m):
        for cp in emb_in[m]:
            cp.wait_recv()
        rest = sum(er[m, q, :, 256:384].astype(F32) for q in range(4))
        wide = jnp.concatenate([er[m, q, :, 0:256].astype(F32) for q in range(4)] + [rest], axis=1)
        scale = lax.rsqrt(jnp.sum(wide * wide, axis=1, keepdims=True) + 1e-06)
        unit[m] = wide * scale
        scal[m] = jnp.broadcast_to(scale, (64, 128))
        return (wide * scale).astype(BF)

    A, B, A0, A1 = pl.ds(0, 32), pl.ds(32, 32), pl.ds(0, 16), pl.ds(16, 16)
    axis1 = ((xp, x2, xm), (yp, y2, ym))
    axis2 = ((yp, y2, ym), (xp, x2, xm))
    got = {}
    piece = normalize(0)
    img[0, 0, 0] = piece[0:32]
    img[0, 1, 0] = piece[32:64]
    for j in (1, 3, 2):
        for h in (0, 1):
            got[0, h, 4 - j] = send(img.at[0, h, 0], img.at[0, h, 4 - j], axis1[h][j - 1])

    def second(j):
        for h in (0, 1):
            got[3, h, j] = send(img.at[0, h, j], img.at[3, h, j], axis2[h][0])
            got[1, h, j] = send(img.at[0, h, j], img.at[1, h, j], axis2[h][2])

    def third(j):
        for h in (0, 1):
            got[3, h, j].wait_recv()
            got[4, h, j] = send(img.at[3, h, j, A0], img.at[2, h, j, A0], axis2[h][0])
            got[1, h, j].wait_recv()
            got[5, h, j] = send(img.at[1, h, j, A1], img.at[2, h, j, A1], axis2[h][2])

    second(0)
    txt[POS[0], 0] = normalize(1)
    tgot = {}
    sgot = []
    tgot[7] = send(txt.at[POS[0], 0], txt.at[POS[7], 0], zp)
    tgot[1] = send(txt.at[POS[0], 0], txt.at[POS[1], 0], zm)
    sgot.append(send(txt.at[POS[0], 0], txt.at[POS[0], 1], sib))

    def text_hop(k):
        for src, nxt, to, half in ((8 - k, 7 - k, zp, A), (k, k + 1, zm, B)):
            tgot[src].wait_recv()
            if k < 3:
                tgot[nxt] = send(txt.at[POS[src], 0], txt.at[POS[nxt], 0], to)
            else:
                tgot[(4, src)] = send(txt.at[POS[src], 0, half], txt.at[POS[4], 0, half], to)
            sgot.append(send(txt.at[POS[src], 0], txt.at[POS[src], 1], sib))

    temp = jnp.exp(jnp.full((1, 1), lt_ref[0], F32))
    shift = jnp.full((1, 1), bs_ref[0], F32)
    gain = temp * (1.0 / total)

    def scores(k, n):
        at = pl.ds(2 * n, 2)
        logits = temp * dot_nt(img[k].reshape(256, 1152), txt[at].reshape(256, 1152)) + shift
        cols = pl.ds(pl.multiple_of(256 * n, 256), 256)
        prob[256 * k:256 * k + 256, cols] = (gain / (1.0 + jnp.exp(-logits))).astype(BF)
        return logits

    def some_scores(k, count):
        def one(i, _):
            scores(k, 3 - i)
            return 0
        lax.fori_loop(0, count, one, 0)

    for j in (1, 3):
        got[0, 0, j].wait_recv()
        got[0, 1, j].wait_recv()
        second(j)
    text_hop(1)
    got[0, 0, 2].wait_recv()
    got[0, 1, 2].wait_recv()
    second(2)
    third(0)
    text_hop(2)
    sgot[1].wait_recv()
    sgot[2].wait_recv()
    scores(0, 3)
    third(1)
    third(3)
    text_hop(3)
    sgot[3].wait_recv()
    sgot[4].wait_recv()
    scores(0, 2)
    third(2)

    for n in (5, 6, 0):
        sgot[n].wait_recv()
    scores(0, 1)
    some_scores(1, 3)
    tgot[(4, 5)].wait_recv()
    tgot[(4, 3)].wait_recv()
    last_sib = send(txt.at[POS[4], 0], txt.at[POS[4], 1], sib)
    some_scores(3, 3)
    last_sib.wait_recv()
    scores(1, 0)
    scores(3, 0)
    logits = scores(0, 0)
    r0 = lax.broadcasted_iota(jnp.int32, (32, 128), 0)
    r1 = lax.broadcasted_iota(jnp.int32, (32, 128), 1)
    for h in (0, 1):
        own = logits[128 * h:128 * h + 32, 128:256]
        prob[128 * h:128 * h + 32, 128:256] = jnp.where(
            r1 == r0 + 32 * h, -gain / (1.0 + jnp.exp(own)), gain / (1.0 + jnp.exp(-own))).astype(BF)

    qa = [[], []]

    def image_block(k):
        gi[k] = dot(prob[256 * k:256 * k + 256, :],
                    txt[...].reshape(1024, 1152)).reshape(2, 4, 32, 1152)
        if k:
            gib[k - 1] = gi[k].astype(BF)
            for h in (0, 1):
                qa[h].append(send(gib.at[k - 1, h], ra.at[k - 1, h], axis2[h][k - 1]))

    def text_block(n):
        gt[2 * n:2 * n + 2] = dot_tn(prob[:, 256 * n:256 * n + 256],
                                     img[...].reshape(1024, 1152)).reshape(2, 2, 64, 1152)
        return send(gt.at[2 * n:2 * n + 2, 1], sibr.at[2 * n:2 * n + 2], sib)

    image_block(1)
    image_block(3)
    for j in range(4):
        for h in (0, 1):
            got[4, h, j].wait_recv()
            got[5, h, j].wait_recv()
    some_scores(2, 4)
    image_block(2)
    q0 = text_block(0)
    q1 = text_block(1)
    q0.wait_recv()
    gtb[POS[4]] = (gt[POS[4], 0] + sibr[POS[4]]).astype(BF)
    plus = send(gtb.at[POS[4], A], tp4.at[A], zp)
    minus = send(gtb.at[POS[4], B], tp4.at[B], zm)
    q2 = text_block(2)
    q3 = text_block(3)
    image_block(0)

    wide_t = jnp.transpose(feats[0])
    for k in range(8):
        featst[0, k] = wide_t[144 * k:144 * k + 144]
    p0 = lax.broadcasted_iota(jnp.int32, (144, 1152), 0)
    at_z = p0 + 126 * ((p0 * 3641) >> 16)
    p1 = lax.broadcasted_iota(jnp.int32, (144, 1152), 1)

    def turn(w, _):
        turned = (p1 == at_z + 18 * w).astype(F32).astype(BF)
        featst[1, w] = dot_nt(turned, feats[1]).astype(BF)
        featst[2, w] = dot_nt(turned, feats[0]).astype(BF)
        return 0
    lax.fori_loop(0, 8, turn, 0)

    q1.wait_recv()
    plus.wait_recv()
    s3 = gt[POS[3], 0] + sibr[POS[3]]
    gtb[POS[3], A] = (s3[0:32] + tp4[A].astype(F32)).astype(BF)
    gtb[POS[3], B] = s3[32:64].astype(BF)
    plus = send(gtb.at[POS[3]], tpr.at[0], zp)
    minus.wait_recv()
    s3 = gt[POS[5], 0] + sibr[POS[5]]
    gtb[POS[5], A] = s3[0:32].astype(BF)
    gtb[POS[5], B] = (s3[32:64] + tp4[B].astype(F32)).astype(BF)
    minus = send(gtb.at[POS[5]], tmr.at[0], zm)

    def text_sum(n, a, b, q, plus, minus):
        q.wait_recv()
        plus.wait_recv()
        gtb[POS[a]] = (gt[POS[a], 0] + sibr[POS[a]] + tpr[n].astype(F32)).astype(BF)
        plus = send(gtb.at[POS[a]], tpr.at[n + 1], zp)
        minus.wait_recv()
        gtb[POS[b]] = (gt[POS[b], 0] + sibr[POS[b]] + tmr[n].astype(F32)).astype(BF)
        return plus, send(gtb.at[POS[b]], tmr.at[n + 1], zm)

    plus, minus = text_sum(0, 2, 6, q2, plus, minus)
    qa2 = []
    for h in (0, 1):
        for cp in qa[h]:
            cp.wait_recv()
        for j in (2, 1, 3, 0):
            part = gi[0, h, j]
            for k in range(3):
                part = part + ra[k, h, j].astype(F32)
            if j:
                sab[h, j - 1] = part.astype(BF)
                qa2.append(send(sab.at[h, j - 1], ra2.at[h, j - 1], axis1[h][j - 1]))
            else:
                sa[h] = part
    plus, minus = text_sum(1, 1, 7, q3, plus, minus)

    def back(m, dx):
        inner = jnp.sum(unit[m] * dx, axis=1, keepdims=True)
        dz = (scal[m][:, 0:1] * (dx - unit[m] * inner)).astype(BF)
        for q in range(4):
            zs[m, q, :, 0:256] = dz[:, 256 * q:256 * q + 256]
            zs[m, q, :, 256:384] = dz[:, 1024:1152]
        zr[m, mp] = zs[m, mp]
        return [send(zs.at[m, (mp + k) % 4], zr.at[m, mp], mps[k - 1]) for k in (1, 2, 3)]

    for cp in qa2:
        cp.wait_recv()
    zi_in = back(0, jnp.concatenate(
        [sa[h] + ra2[h, 0].astype(F32) + ra2[h, 1].astype(F32) + ra2[h, 2].astype(F32)
         for h in (0, 1)], axis=0))
    plus.wait_recv()
    minus.wait_recv()
    zt_in = back(1, gt[POS[0], 0] + sibr[POS[0]] + tpr[2].astype(F32) + tmr[2].astype(F32))

    far_z, far_w = (4, 3, 5, 2, 6, 1, 7), (6, 2, 5, 7, 1, 3, 4)
    l0 = lax.broadcasted_iota(jnp.int32, (128, 128), 0)
    l1 = lax.broadcasted_iota(jnp.int32, (128, 128), 1)

    def by_z(k):
        return (z + k) % 8

    def by_w(k):
        return ((xl + k // 4) % 2) * 4 + (y + k) % 4

    def columns(m, arrived):
        for cp in arrived:
            cp.wait_recv()
        pick = ((l0 + 32 * m == l1 + 32 * mp) & (l1 >= 32 * m) & (l1 < 32 * m + 32)).astype(F32).astype(BF)
        rest = jnp.concatenate([zr[m, q, :, 256:384] for q in range(4)], axis=0)
        return (jnp.concatenate([zr[m, q, :, 0:256] for q in range(4)], axis=0),
                dot(rest, pick).astype(BF))

    def spread(st, rc, far, make, at):
        q = []
        for k in far:
            st[k] = make(k).astype(BF)
            q.append(send(st.at[k], rc.at[k], at[k]))
        return q

    def regroup(q, own, rc, far, ys, yr, base, at):
        for cp in q:
            cp.wait_recv()
        for k in far:
            own = own + rc[k].astype(F32)
        for k in range(8):
            ys[k, 0:18] = own[18 * k:18 * k + 18]
        return [send(ys.at[base(k)], yr.at[k], at[k]) for k in far]

    def last_sum(q, ys, yr, base):
        for cp in q:
            cp.wait_recv()
        out = ys[base(0)]
        for k in range(1, 8):
            out = out + yr[k]
        return out

    main_i, rest_i = columns(0, zi_in)

    def make_i(k):
        return dot(featst[0, by_z(k)], main_i)

    qi = spread(fsi, fri, far_z, make_i, zs_at)
    own_i = make_i(0)
    main_t, rest_t = columns(1, zt_in)

    def make_t(k):
        a, b = featst[1, by_w(k)], featst[2, by_w(k)]
        return jnp.concatenate([dot(a, main_t), dot(a, rest_t) + dot(b, rest_i)], axis=1)

    qt = spread(fst, frt, far_w, make_t, ws_at)
    own_t = make_t(0)
    qi = regroup(qi, own_i, fri, far_z, ysi, yri, by_w, ws_at)
    qt = regroup(qt, own_t, frt, far_w, yst, yrt, by_z, zs_at)
    oi_ref[:, 0:256] = last_sum(qi, ysi, yri, by_w)[0:18]
    out = last_sum(qt, yst, yrt, by_z)
    ot_ref[:, 0:256] = out[0:18, 0:256]
    oi_ref[:, 256:288] = out[0:18, 256:288]
    ot_ref[:, 256:288] = pltpu.roll(out[:, 256:384], 96, 1)[0:18, 0:32]
    for cp in started:
        cp.wait_send()


COPIES = 256


def local(image_feats, text_feats, image_proj, text_proj, log_temp, bias):
    total = image_feats.shape[0] * lax.axis_size("dp")
    vm = pltpu.VMEM
    out = jax.ShapeDtypeStruct((18, 288), F32)
    return pl.pallas_call(
        functools.partial(kernel, total),
        out_shape=(out, out),
        in_specs=[pl.BlockSpec(memory_space=pl.ANY)] * 4
        + [pl.BlockSpec(memory_space=pltpu.SMEM)] * 2,
        out_specs=(pl.BlockSpec(memory_space=vm), pl.BlockSpec(memory_space=vm)),
        scratch_shapes=[
            vm((2, 256, 1152), BF),
            vm((2, 288, 1152), BF),
            vm((3, 8, 144, 256), BF),
            vm((2, 4, 64, 384), BF),
            vm((2, 4, 64, 384), BF),
            vm((2, 64, 1152), F32),
            vm((2, 64, 128), F32),
            vm((4, 2, 4, 32, 1152), BF),
            vm((8, 2, 64, 1152), BF),
            vm((1024, 1024), BF),
            vm((4, 2, 4, 32, 1152), F32),
            vm((8, 2, 64, 1152), F32),
            vm((3, 2, 4, 32, 1152), BF),
            vm((3, 2, 4, 32, 1152), BF),
            vm((2, 3, 32, 1152), BF),
            vm((2, 32, 1152), F32),
            vm((2, 3, 32, 1152), BF),
            vm((8, 64, 1152), F32),
            vm((8, 64, 1152), BF),
            vm((64, 1152), BF),
            vm((3, 64, 1152), BF),
            vm((3, 64, 1152), BF),
            vm((2, 4, 64, 384), BF),
            vm((2, 4, 64, 384), BF),
            vm((8, 144, 256), BF),
            vm((8, 144, 256), BF),
            vm((8, 144, 384), BF),
            vm((8, 144, 384), BF),
            vm((8, 24, 256), F32),
            vm((8, 24, 256), F32),
            vm((8, 24, 384), F32),
            vm((8, 24, 384), F32),
            pltpu.SemaphoreType.DMA((4,)),
            pltpu.SemaphoreType.DMA((COPIES,)),
            pltpu.SemaphoreType.DMA((COPIES,)),
        ],
        name="contrastive",
        compiler_params=pltpu.CompilerParams(
            collective_id=0, has_side_effects=True, vmem_limit_bytes=60 * 2**20
        ),
    )(image_feats, text_feats, image_proj.T, text_proj.T, log_temp, bias)


def solution(mesh):
    placed = (P("dp", None), P("dp", None), P(None, "mp"), P(None, "mp"), P(), P())
    return jax.shard_map(
        local, mesh=mesh, in_specs=placed, out_specs=(P("dp", "mp"), P("dp", "mp")), check_vma=False
    )
```

time: 111 us -> 100 us (0.901)
  Pallas kernels: 105 us -> 95.4 us
    pallas_call x1, Pallas kernels: 105 us -> 95.4 us  [local(): pl.pallas_call(functools.partial(kernel, total), out_shape=(out, out), in...]
where the time goes in v3:
time: 100 us; the launch traced here: 99.4 us
  Pallas kernels  95.4 us (95%)
  local copies, waits for them, and re-layouts  2.01 us (2%)
  between operations  1.94 us (2%)
    pallas_call x1, Pallas kernels, local(): pl.pallas_call(functools.partial(kernel, total), out_shape=(out, out), in...  95.4 us
    unnamed x4, local copies, waits for them, and re-layouts  2.01 us

profile of v3, /device:TPU:2, one launch (start us, length us, event | category | flops | bytes accessed | tf_op | source)
XLA Modules:
  0.0 99.4 jit_solution(8755142060071145171)
XLA Ops:
  1.9 95.4 %contrastive.1 = (f32[18,288]{1,0:T(8,128)}, f32[18,288]{1,0:T(8,128)}) custom-call(bf16[224,1152]{1,0:T(8,128)(2,1)} %fi_hbm.1, bf16[224,1152]{1,0:T(8,128)(2,1)} %ft_hbm.1, bf16[288,1152]{1,0:T(8,128)(2,1)} %bitcast.2, bf16[288,1152]{1,0:T(8,128)(2,1)} %bitcast.3, f32[1]{0:T(128)S(6)} %copy.10.lt_ref, f32[1]{0:T(128)S(6)} %copy.11.bs_ref), custom_call_target="tpu_custom_call" | custom-call | tf_op jit(solution)/shard_map/contrastive/pallas_call | solution.py:374
  97.4 0.0 copy-start
  97.4 1.4 %copy.12 = f32[18,288]{1,0:T(8,128)} copy(f32[18,288]{1,0:T(8,128)} %get-tuple-element.4) | data formatting | bytes 41472
  98.8 0.0 copy-done
  98.8 0.6 copy.13
Async XLA Ops:
  97.4 1.4 %copy-start = (f32[18,288]{1,0:T(8,128)S(1)}, f32[18,288]{1,0:T(8,128)}, u32[]{:S(2)}) copy-start(f32[18,288]{1,0:T(8,128)} %get-tuple-element.5) | copy-start | bytes 62212

commit v4 on v3

--- a/solution.py
+++ b/solution.py
@@ -27,7 +27,7 @@
 
 def kernel(total, fi_hbm, ft_hbm, wi_hbm, wt_hbm, lt_ref, bs_ref, oi_ref, ot_ref,
            feats, wts, featst, es, er, unit, scal, img, txt, prob, gi, gt,
-           gib, ra, ra2, sa, sab, sibr, gtb, tp4, tpr, tmr, zs, zr,
+           gib, ra, ra2, r4, sa, sab, gts, sibr, gtb, tr, zs, zr,
            fsi, fri, fst, frt, ysi, yri, yst, yrt,
            lsem, ssem, rsem):
     dp, mp = lax.axis_index("dp"), lax.axis_index("mp")
@@ -122,21 +122,34 @@
 
     second(0)
     txt[POS[0], 0] = normalize(1)
-    tgot = {}
-    sgot = []
-    tgot[7] = send(txt.at[POS[0], 0], txt.at[POS[7], 0], zp)
-    tgot[1] = send(txt.at[POS[0], 0], txt.at[POS[1], 0], zm)
-    sgot.append(send(txt.at[POS[0], 0], txt.at[POS[0], 1], sib))
+    tgot, sgot = {}, {}
+    halves = (A, B)
+
+    def text_send(src, dst, half, to):
+        tgot[dst, half] = send(txt.at[POS[src], 0, halves[half]], txt.at[POS[dst], 0, halves[half]], to)
+
+    def text_share(*slots):
+        for k in slots:
+            sgot[k] = send(txt.at[POS[k], 0], txt.at[POS[k], 1], sib)
+
+    def text_shared(*slots):
+        for k in slots:
+            sgot[k].wait_recv()
 
     def text_hop(k):
-        for src, nxt, to, half in ((8 - k, 7 - k, zp, A), (k, k + 1, zm, B)):
-            tgot[src].wait_recv()
-            if k < 3:
-                tgot[nxt] = send(txt.at[POS[src], 0], txt.at[POS[nxt], 0], to)
-            else:
-                tgot[(4, src)] = send(txt.at[POS[src], 0, half], txt.at[POS[4], 0, half], to)
-            sgot.append(send(txt.at[POS[src], 0], txt.at[POS[src], 1], sib))
-
+        for turn in (0, 1):
+            for src, nxt, to, lead in ((8 - k, 7 - k, zp, 0), (k, k + 1, zm, 1)):
+                half = (lead + turn) % 2
+                tgot[src, half].wait_recv()
+                if k < 3 or turn == 0:
+                    text_send(src, nxt, half, to)
+        text_share(8 - k, k)
+
+    text_send(0, 7, 0, zp)
+    text_send(0, 1, 1, zm)
+    text_send(0, 7, 1, zp)
+    text_send(0, 1, 0, zm)
+    text_share(0)
     temp = jnp.exp(jnp.full((1, 1), lt_ref[0], F32))
     shift = jnp.full((1, 1), bs_ref[0], F32)
     gain = temp * (1.0 / total)
@@ -153,6 +166,32 @@
             scores(k, 3 - i)
             return 0
         lax.fori_loop(0, count, one, 0)
+
+    sent = {}
+
+    def image_block(k):
+        gi[k] = dot(prob[256 * k:256 * k + 256, :],
+                    txt[...].reshape(1024, 1152)).reshape(2, 4, 32, 1152)
+
+    def text_block(n):
+        gt[2 * n:2 * n + 2] = dot_tn(prob[:, 256 * n:256 * n + 256],
+                                     img[...].reshape(1024, 1152)).reshape(2, 2, 64, 1152)
+        gts[n] = gt[2 * n:2 * n + 2, 1].astype(BF)
+        return send(gts.at[n], sibr.at[n], sib)
+
+    def text_own(k):
+        return gt[POS[k], 0] + sibr[POS[k] // 2, POS[k] % 2].astype(F32)
+
+    def text_on(k, half):
+        at = halves[half]
+        part = gt[POS[k], 0, at] + sibr[POS[k] // 2, POS[k] % 2, at].astype(F32)
+        back_k = k + 1 if k < 4 else k - 1
+        if k != 4 and (back_k != 4 or half == (0 if k == 3 else 1)):
+            sent[back_k, half].wait_recv()
+            part = part + tr[back_k, at].astype(F32)
+        gtb[k, at] = part.astype(BF)
+        to = zp if k < 4 or (k == 4 and half == 0) else zm
+        sent[k, half] = send(gtb.at[k, at], tr.at[k, at], to)
 
     for j in (1, 3):
         got[0, 0, j].wait_recv()
@@ -164,26 +203,30 @@
     second(2)
     third(0)
     text_hop(2)
-    sgot[1].wait_recv()
-    sgot[2].wait_recv()
+    text_shared(1, 7)
     scores(0, 3)
     third(1)
     third(3)
     text_hop(3)
-    sgot[3].wait_recv()
-    sgot[4].wait_recv()
+    text_shared(2, 6)
     scores(0, 2)
     third(2)
 
-    for n in (5, 6, 0):
-        sgot[n].wait_recv()
-    scores(0, 1)
-    some_scores(1, 3)
-    tgot[(4, 5)].wait_recv()
-    tgot[(4, 3)].wait_recv()
-    last_sib = send(txt.at[POS[4], 0], txt.at[POS[4], 1], sib)
-    some_scores(3, 3)
-    last_sib.wait_recv()
+    def two_scores(k):
+        def one(i, _):
+            scores(k, 3 - i)
+            return 0
+        lax.fori_loop(0, 2, one, 0)
+
+    two_scores(1)
+    tgot[4, 0].wait_recv()
+    tgot[4, 1].wait_recv()
+    text_share(4)
+    two_scores(3)
+    text_shared(3, 5, 0)
+    for k in (1, 3, 0):
+        scores(k, 1)
+    text_shared(4)
     scores(1, 0)
     scores(3, 0)
     logits = scores(0, 0)
@@ -194,89 +237,62 @@
         prob[128 * h:128 * h + 32, 128:256] = jnp.where(
             r1 == r0 + 32 * h, -gain / (1.0 + jnp.exp(own)), gain / (1.0 + jnp.exp(-own))).astype(BF)
 
-    qa = [[], []]
-
-    def image_block(k):
-        gi[k] = dot(prob[256 * k:256 * k + 256, :],
-                    txt[...].reshape(1024, 1152)).reshape(2, 4, 32, 1152)
-        if k:
-            gib[k - 1] = gi[k].astype(BF)
-            for h in (0, 1):
-                qa[h].append(send(gib.at[k - 1, h], ra.at[k - 1, h], axis2[h][k - 1]))
-
-    def text_block(n):
-        gt[2 * n:2 * n + 2] = dot_tn(prob[:, 256 * n:256 * n + 256],
-                                     img[...].reshape(1024, 1152)).reshape(2, 2, 64, 1152)
-        return send(gt.at[2 * n:2 * n + 2, 1], sibr.at[2 * n:2 * n + 2], sib)
-
-    image_block(1)
-    image_block(3)
     for j in range(4):
         for h in (0, 1):
             got[4, h, j].wait_recv()
             got[5, h, j].wait_recv()
     some_scores(2, 4)
     image_block(2)
+    gib[1] = gi[2].astype(BF)
+    q4 = [[send(gib.at[1, h, :, A0], r4.at[h, :, A0], axis2[h][0]),
+           send(gib.at[1, h, :, A1], r4.at[h, :, A1], axis2[h][2])] for h in (0, 1)]
     q0 = text_block(0)
+    image_block(1)
+    image_block(3)
+    for h in (0, 1):
+        gib[0, h, :, A1] = gi[1, h, :, A1].astype(BF)
+        gib[2, h, :, A0] = gi[3, h, :, A0].astype(BF)
     q1 = text_block(1)
     q0.wait_recv()
-    gtb[POS[4]] = (gt[POS[4], 0] + sibr[POS[4]]).astype(BF)
-    plus = send(gtb.at[POS[4], A], tp4.at[A], zp)
-    minus = send(gtb.at[POS[4], B], tp4.at[B], zm)
+    text_on(4, 0)
+    text_on(4, 1)
+    q1.wait_recv()
+    text_on(3, 1)
+    text_on(5, 0)
+    qa = [[], []]
+    for h in (0, 1):
+        for cp in q4[h]:
+            cp.wait_recv()
+        gib[0, h, :, A0] = (gi[1, h, :, A0] + r4[h, :, A0].astype(F32)).astype(BF)
+        gib[2, h, :, A1] = (gi[3, h, :, A1] + r4[h, :, A1].astype(F32)).astype(BF)
+        for i in (0, 1):
+            qa[h].append(send(gib.at[2 * i, h], ra.at[i, h], axis2[h][2 * i]))
     q2 = text_block(2)
     q3 = text_block(3)
+    text_on(3, 0)
+    text_on(5, 1)
     image_block(0)
-
-    wide_t = jnp.transpose(feats[0])
-    for k in range(8):
-        featst[0, k] = wide_t[144 * k:144 * k + 144]
-    p0 = lax.broadcasted_iota(jnp.int32, (144, 1152), 0)
-    at_z = p0 + 126 * ((p0 * 3641) >> 16)
-    p1 = lax.broadcasted_iota(jnp.int32, (144, 1152), 1)
-
-    def turn(w, _):
-        turned = (p1 == at_z + 18 * w).astype(F32).astype(BF)
-        featst[1, w] = dot_nt(turned, feats[1]).astype(BF)
-        featst[2, w] = dot_nt(turned, feats[0]).astype(BF)
-        return 0
-    lax.fori_loop(0, 8, turn, 0)
-
-    q1.wait_recv()
-    plus.wait_recv()
-    s3 = gt[POS[3], 0] + sibr[POS[3]]
-    gtb[POS[3], A] = (s3[0:32] + tp4[A].astype(F32)).astype(BF)
-    gtb[POS[3], B] = s3[32:64].astype(BF)
-    plus = send(gtb.at[POS[3]], tpr.at[0], zp)
-    minus.wait_recv()
-    s3 = gt[POS[5], 0] + sibr[POS[5]]
-    gtb[POS[5], A] = s3[0:32].astype(BF)
-    gtb[POS[5], B] = (s3[32:64] + tp4[B].astype(F32)).astype(BF)
-    minus = send(gtb.at[POS[5]], tmr.at[0], zm)
-
-    def text_sum(n, a, b, q, plus, minus):
-        q.wait_recv()
-        plus.wait_recv()
-        gtb[POS[a]] = (gt[POS[a], 0] + sibr[POS[a]] + tpr[n].astype(F32)).astype(BF)
-        plus = send(gtb.at[POS[a]], tpr.at[n + 1], zp)
-        minus.wait_recv()
-        gtb[POS[b]] = (gt[POS[b], 0] + sibr[POS[b]] + tmr[n].astype(F32)).astype(BF)
-        return plus, send(gtb.at[POS[b]], tmr.at[n + 1], zm)
-
-    plus, minus = text_sum(0, 2, 6, q2, plus, minus)
+    q2.wait_recv()
+    text_on(2, 1)
+    text_on(6, 0)
+    text_on(2, 0)
+    text_on(6, 1)
+    q3.wait_recv()
+    text_on(1, 1)
+    text_on(7, 0)
     qa2 = []
     for h in (0, 1):
         for cp in qa[h]:
             cp.wait_recv()
         for j in (2, 1, 3, 0):
-            part = gi[0, h, j]
-            for k in range(3):
-                part = part + ra[k, h, j].astype(F32)
+            part = gi[0, h, j] + ra[0, h, j].astype(F32) + ra[1, h, j].astype(F32)
             if j:
                 sab[h, j - 1] = part.astype(BF)
                 qa2.append(send(sab.at[h, j - 1], ra2.at[h, j - 1], axis1[h][j - 1]))
             else:
                 sa[h] = part
-    plus, minus = text_sum(1, 1, 7, q3, plus, minus)
+    text_on(1, 0)
+    text_on(7, 1)
 
     def back(m, dx):
         inner = jnp.sum(unit[m] * dx, axis=1, keepdims=True)
@@ -287,14 +303,30 @@
         zr[m, mp] = zs[m, mp]
         return [send(zs.at[m, (mp + k) % 4], zr.at[m, mp], mps[k - 1]) for k in (1, 2, 3)]
 
+    for k in (1, 7):
+        for half in (0, 1):
+            sent[k, half].wait_recv()
+    zt_in = back(1, text_own(0) + tr[1].astype(F32) + tr[7].astype(F32))
     for cp in qa2:
         cp.wait_recv()
     zi_in = back(0, jnp.concatenate(
         [sa[h] + ra2[h, 0].astype(F32) + ra2[h, 1].astype(F32) + ra2[h, 2].astype(F32)
          for h in (0, 1)], axis=0))
-    plus.wait_recv()
-    minus.wait_recv()
-    zt_in = back(1, gt[POS[0], 0] + sibr[POS[0]] + tpr[2].astype(F32) + tmr[2].astype(F32))
+
+    wide_t = jnp.transpose(feats[0])
+    for k in range(8):
+        featst[0, k] = wide_t[144 * k:144 * k + 144]
+    p0 = lax.broadcasted_iota(jnp.int32, (144, 1152), 0)
+    at_z = p0 + 126 * ((p0 * 3641) >> 16)
+    p1 = lax.broadcasted_iota(jnp.int32, (144, 1152), 1)
+
+    def turn(w, _):
+        turned = (p1 == at_z + 18 * w).astype(F32).astype(BF)
+        featst[1, w] = dot_nt(turned, feats[1]).astype(BF)
+        featst[2, w] = dot_nt(turned, feats[0]).astype(BF)
+        return 0
+    lax.fori_loop(0, 8, turn, 0)
+
 
     far_z, far_w = (4, 3, 5, 2, 6, 1, 7), (6, 2, 5, 7, 1, 3, 4)
     l0 = lax.broadcasted_iota(jnp.int32, (128, 128), 0)
@@ -327,15 +359,15 @@
         for k in far:
             own = own + rc[k].astype(F32)
         for k in range(8):
-            ys[k, 0:18] = own[18 * k:18 * k + 18]
+            ys[k, 0:18] = own[18 * k:18 * k + 18].astype(BF)
         return [send(ys.at[base(k)], yr.at[k], at[k]) for k in far]
 
     def last_sum(q, ys, yr, base):
         for cp in q:
             cp.wait_recv()
-        out = ys[base(0)]
+        out = ys[base(0)].astype(F32)
         for k in range(1, 8):
-            out = out + yr[k]
+            out = out + yr[k].astype(F32)
         return out
 
     main_i, rest_i = columns(0, zi_in)
@@ -391,25 +423,25 @@
             vm((4, 2, 4, 32, 1152), F32),
             vm((8, 2, 64, 1152), F32),
             vm((3, 2, 4, 32, 1152), BF),
-            vm((3, 2, 4, 32, 1152), BF),
+            vm((2, 2, 4, 32, 1152), BF),
             vm((2, 3, 32, 1152), BF),
+            vm((2, 4, 32, 1152), BF),
             vm((2, 32, 1152), F32),
             vm((2, 3, 32, 1152), BF),
-            vm((8, 64, 1152), F32),
+            vm((4, 2, 64, 1152), BF),
+            vm((4, 2, 64, 1152), BF),
             vm((8, 64, 1152), BF),
-            vm((64, 1152), BF),
-            vm((3, 64, 1152), BF),
-            vm((3, 64, 1152), BF),
+            vm((8, 64, 1152), BF),
             vm((2, 4, 64, 384), BF),
             vm((2, 4, 64, 384), BF),
             vm((8, 144, 256), BF),
             vm((8, 144, 256), BF),
             vm((8, 144, 384), BF),
             vm((8, 144, 384), BF),
-            vm((8, 24, 256), F32),
-            vm((8, 24, 256), F32),
-            vm((8, 24, 384), F32),
-            vm((8, 24, 384), F32),
+            vm((8, 32, 256), BF),
+            vm((8, 32, 256), BF),
+            vm((8, 32, 384), BF),
+            vm((8, 32, 384), BF),
             pltpu.SemaphoreType.DMA((4,)),
             pltpu.SemaphoreType.DMA((COPIES,)),
             pltpu.SemaphoreType.DMA((COPIES,)),

time: 100 us -> 94.9 us (0.949)
  Pallas kernels: 95.4 us -> 90.8 us
    pallas_call x1, Pallas kernels: 95.4 us -> 90.8 us  [local(): pl.pallas_call(functools.partial(kernel, total), out_shape=(out, out), in...]
where the time goes in v4:
time: 94.9 us; the launch traced here: 94.7 us
  Pallas kernels  90.8 us (96%)
  local copies, waits for them, and re-layouts  2.01 us (2%)
  between operations  1.94 us (2%)
    pallas_call x1, Pallas kernels, local(): pl.pallas_call(functools.partial(kernel, total), out_shape=(out, out), in...  90.8 us
    unnamed x4, local copies, waits for them, and re-layouts  2.01 us

profile of v4, /device:TPU:2, one launch (start us, length us, event | category | flops | bytes accessed | tf_op | source)
XLA Modules:
  0.0 94.7 jit_solution(5096307395598105582)
XLA Ops:
  1.9 90.8 %contrastive.1 = (f32[18,288]{1,0:T(8,128)}, f32[18,288]{1,0:T(8,128)}) custom-call(bf16[224,1152]{1,0:T(8,128)(2,1)} %fi_hbm.1, bf16[224,1152]{1,0:T(8,128)(2,1)} %ft_hbm.1, bf16[288,1152]{1,0:T(8,128)(2,1)} %bitcast.2, bf16[288,1152]{1,0:T(8,128)(2,1)} %bitcast.3, f32[1]{0:T(128)S(6)} %copy.10.lt_ref, f32[1]{0:T(128)S(6)} %copy.11.bs_ref), custom_call_target="tpu_custom_call" | custom-call | tf_op jit(solution)/shard_map/contrastive/pallas_call | solution.py:406
  92.7 0.0 copy-start
  92.7 1.4 %copy.12 = f32[18,288]{1,0:T(8,128)} copy(f32[18,288]{1,0:T(8,128)} %get-tuple-element.4) | data formatting | bytes 41472
  94.1 0.0 copy-done
  94.1 0.6 copy.13
Async XLA Ops:
  92.7 1.4 %copy-start = (f32[18,288]{1,0:T(8,128)S(1)}, f32[18,288]{1,0:T(8,128)}, u32[]{:S(2)}) copy-start(f32[18,288]{1,0:T(8,128)} %get-tuple-element.5) | copy-start | bytes 62212

commit v5 on v4

--- a/solution.py
+++ b/solution.py
@@ -28,7 +28,7 @@
 def kernel(total, fi_hbm, ft_hbm, wi_hbm, wt_hbm, lt_ref, bs_ref, oi_ref, ot_ref,
            feats, wts, featst, es, er, unit, scal, img, txt, prob, gi, gt,
            gib, ra, ra2, r4, sa, sab, gts, sibr, gtb, tr, zs, zr,
-           fsi, fri, fst, frt, ysi, yri, yst, yrt,
+           fsi, fri, fst, frt, fsr, frr, ysi, yri, yst, yrt,
            lsem, ssem, rsem):
     dp, mp = lax.axis_index("dp"), lax.axis_index("mp")
     z, xl, y = dp // 8, (dp // 4) % 2, dp % 4
@@ -136,14 +136,15 @@
         for k in slots:
             sgot[k].wait_recv()
 
-    def text_hop(k):
-        for turn in (0, 1):
+    def text_hop(k, turns=(0, 1)):
+        for turn in turns:
             for src, nxt, to, lead in ((8 - k, 7 - k, zp, 0), (k, k + 1, zm, 1)):
                 half = (lead + turn) % 2
                 tgot[src, half].wait_recv()
                 if k < 3 or turn == 0:
                     text_send(src, nxt, half, to)
-        text_share(8 - k, k)
+        if turns[-1]:
+            text_share(8 - k, k)
 
     text_send(0, 7, 0, zp)
     text_send(0, 1, 1, zm)
@@ -207,10 +208,10 @@
     scores(0, 3)
     third(1)
     third(3)
-    text_hop(3)
     text_shared(2, 6)
     scores(0, 2)
     third(2)
+    text_hop(3, (0,))
 
     def two_scores(k):
         def one(i, _):
@@ -219,10 +220,11 @@
         lax.fori_loop(0, 2, one, 0)
 
     two_scores(1)
+    text_hop(3, (1,))
+    two_scores(3)
     tgot[4, 0].wait_recv()
     tgot[4, 1].wait_recv()
     text_share(4)
-    two_scores(3)
     text_shared(3, 5, 0)
     for k in (1, 3, 0):
         scores(k, 1)
@@ -242,55 +244,68 @@
             got[4, h, j].wait_recv()
             got[5, h, j].wait_recv()
     some_scores(2, 4)
+    q0 = text_block(0)
     image_block(2)
     gib[1] = gi[2].astype(BF)
-    q4 = [[send(gib.at[1, h, :, A0], r4.at[h, :, A0], axis2[h][0]),
-           send(gib.at[1, h, :, A1], r4.at[h, :, A1], axis2[h][2])] for h in (0, 1)]
-    q0 = text_block(0)
-    image_block(1)
-    image_block(3)
-    for h in (0, 1):
-        gib[0, h, :, A1] = gi[1, h, :, A1].astype(BF)
-        gib[2, h, :, A0] = gi[3, h, :, A0].astype(BF)
+    pairs = (pl.ds(2, 2), pl.ds(0, 2))
+    q4 = [[[send(gib.at[1, h, p, A0], r4.at[h, p, A0], axis2[h][0]),
+            send(gib.at[1, h, p, A1], r4.at[h, p, A1], axis2[h][2])] for h in (0, 1)] for p in pairs]
     q1 = text_block(1)
     q0.wait_recv()
     text_on(4, 0)
     text_on(4, 1)
+    image_block(1)
+    for h in (0, 1):
+        gib[0, h, :, A1] = gi[1, h, :, A1].astype(BF)
     q1.wait_recv()
     text_on(3, 1)
     text_on(5, 0)
+    image_block(3)
+    for h in (0, 1):
+        gib[2, h, :, A0] = gi[3, h, :, A0].astype(BF)
     qa = [[], []]
-    for h in (0, 1):
-        for cp in q4[h]:
+
+    def image_on(n):
+        p = pairs[n]
+        for h in (0, 1):
+            for cp in q4[n][h]:
+                cp.wait_recv()
+            gib[0, h, p, A0] = (gi[1, h, p, A0] + r4[h, p, A0].astype(F32)).astype(BF)
+            gib[2, h, p, A1] = (gi[3, h, p, A1] + r4[h, p, A1].astype(F32)).astype(BF)
+            for i in (0, 1):
+                qa[n].append(send(gib.at[2 * i, h, p], ra.at[i, h, p], axis2[h][2 * i]))
+
+    qa2 = []
+
+    def image_first(n):
+        for cp in qa[n]:
             cp.wait_recv()
-        gib[0, h, :, A0] = (gi[1, h, :, A0] + r4[h, :, A0].astype(F32)).astype(BF)
-        gib[2, h, :, A1] = (gi[3, h, :, A1] + r4[h, :, A1].astype(F32)).astype(BF)
-        for i in (0, 1):
-            qa[h].append(send(gib.at[2 * i, h], ra.at[i, h], axis2[h][2 * i]))
+        for j in (2, 3) if n == 0 else (1, 0):
+            for h in (0, 1):
+                part = gi[0, h, j] + ra[0, h, j].astype(F32) + ra[1, h, j].astype(F32)
+                if j:
+                    sab[h, j - 1] = part.astype(BF)
+                    qa2.append(send(sab.at[h, j - 1], ra2.at[h, j - 1], axis1[h][j - 1]))
+                else:
+                    sa[h] = part
+
+    image_on(0)
     q2 = text_block(2)
-    q3 = text_block(3)
     text_on(3, 0)
     text_on(5, 1)
+    image_on(1)
+    q3 = text_block(3)
     image_block(0)
     q2.wait_recv()
     text_on(2, 1)
     text_on(6, 0)
     text_on(2, 0)
     text_on(6, 1)
+    image_first(0)
     q3.wait_recv()
     text_on(1, 1)
     text_on(7, 0)
-    qa2 = []
-    for h in (0, 1):
-        for cp in qa[h]:
-            cp.wait_recv()
-        for j in (2, 1, 3, 0):
-            part = gi[0, h, j] + ra[0, h, j].astype(F32) + ra[1, h, j].astype(F32)
-            if j:
-                sab[h, j - 1] = part.astype(BF)
-                qa2.append(send(sab.at[h, j - 1], ra2.at[h, j - 1], axis1[h][j - 1]))
-            else:
-                sa[h] = part
+    image_first(1)
     text_on(1, 0)
     text_on(7, 1)
 
@@ -346,20 +361,17 @@
         return (jnp.concatenate([zr[m, q, :, 0:256] for q in range(4)], axis=0),
                 dot(rest, pick).astype(BF))
 
-    def spread(st, rc, far, make, at):
-        q = []
-        for k in far:
-            st[k] = make(k).astype(BF)
-            q.append(send(st.at[k], rc.at[k], at[k]))
-        return q
-
-    def regroup(q, own, rc, far, ys, yr, base, at):
+    def regroup(q, own, rc, near, far, ys, yr, base, at):
         for cp in q:
             cp.wait_recv()
-        for k in far:
+        for k in near:
             own = own + rc[k].astype(F32)
+        cols = own.shape[1]
         for k in range(8):
-            ys[k, 0:18] = own[18 * k:18 * k + 18].astype(BF)
+            ys[k, :, 0:cols] = own[18 * k:18 * k + 16].astype(BF)
+            tail = [own[18 * k + r:18 * k + r + 1, i:i + 128] for r in (16, 17) for i in range(0, cols, 128)]
+            tail.append(jnp.zeros((16 - len(tail), 128), F32))
+            ys[k, :, cols:cols + 128] = jnp.concatenate(tail, axis=0).astype(BF)
         return [send(ys.at[base(k)], yr.at[k], at[k]) for k in far]
 
     def last_sum(q, ys, yr, base):
@@ -368,30 +380,65 @@
         out = ys[base(0)].astype(F32)
         for k in range(1, 8):
             out = out + yr[k].astype(F32)
-        return out
+        cols = out.shape[1] - 128
+        n = cols // 128
+        tail = [jnp.concatenate([out[r * n + i:r * n + i + 1, cols:] for i in range(n)], axis=1) for r in (0, 1)]
+        return jnp.concatenate([out[:, 0:cols]] + tail, axis=0)
 
     main_i, rest_i = columns(0, zi_in)
+    main_t, rest_t = columns(1, zt_in)
+
+    def make_t(k):
+        a, b = featst[1, by_w(k)], featst[2, by_w(k)]
+        rest = dot(a, rest_t) + dot(b, rest_i)
+        return dot(a, main_t), rest[0:72] + pltpu.roll(rest[72:144], 64, 1)
+
+    qt = []
+    for k in far_w:
+        part, rest = make_t(k)
+        fst[k] = part.astype(BF)
+        fsr[k, 0:72] = rest.astype(BF)
+        qt.append(send(fst.at[k], frt.at[k], ws_at[k]))
+        qt.append(send(fsr.at[k], frr.at[k], ws_at[k]))
+    own_t, own_r = make_t(0)
+
 
     def make_i(k):
         return dot(featst[0, by_z(k)], main_i)
 
-    qi = spread(fsi, fri, far_z, make_i, zs_at)
+    H0, H1 = pl.ds(0, 80), pl.ds(80, 64)
+    fsi[4] = make_i(4).astype(BF)
+    qi4 = [send(fsi.at[4, H0], fri.at[4, H0], zs_at[2]), send(fsi.at[4, H1], fri.at[4, H1], zs_at[6])]
+    qi3, qi = [], []
+    for k, q in ((3, qi3), (5, qi3), (1, qi), (7, qi)):
+        fsi[k] = make_i(k).astype(BF)
+        q.append(send(fsi.at[k], fri.at[k], zp if k < 4 else zm))
+    own_2, own_6 = make_i(2), make_i(6)
     own_i = make_i(0)
-    main_t, rest_t = columns(1, zt_in)
-
-    def make_t(k):
-        a, b = featst[1, by_w(k)], featst[2, by_w(k)]
-        return jnp.concatenate([dot(a, main_t), dot(a, rest_t) + dot(b, rest_i)], axis=1)
-
-    qt = spread(fst, frt, far_w, make_t, ws_at)
-    own_t = make_t(0)
-    qi = regroup(qi, own_i, fri, far_z, ysi, yri, by_w, ws_at)
-    qt = regroup(qt, own_t, frt, far_w, yst, yrt, by_z, zs_at)
-    oi_ref[:, 0:256] = last_sum(qi, ysi, yri, by_w)[0:18]
+    for k, part, via, half in ((2, own_2, 3, 0), (6, own_6, 5, 1)):
+        qi3[half].wait_recv()
+        part = part + fri[via].astype(F32)
+        qi4[half].wait_recv()
+        if half == 0:
+            fsi[k, H0] = (part[0:80] + fri[4, H0].astype(F32)).astype(BF)
+            fsi[k, H1] = part[80:144].astype(BF)
+        else:
+            fsi[k, H0] = part[0:80].astype(BF)
+            fsi[k, H1] = (part[80:144] + fri[4, H1].astype(F32)).astype(BF)
+        qi.append(send(fsi.at[k], fri.at[k], zs_at[k]))
+    for cp in qt:
+        cp.wait_recv()
+    for k in far_w:
+        own_r = own_r + frr[k, 0:72].astype(F32)
+        own_t = own_t + frt[k].astype(F32)
+    own_t = jnp.concatenate([own_t, jnp.concatenate([own_r, pltpu.roll(own_r, 64, 1)], axis=0)], axis=1)
+    qt = regroup([], own_t, frt, (), far_z, yst, yrt, by_z, zs_at)
+    qi = regroup(qi, own_i, fri, (1, 7, 2, 6), far_w, ysi, yri, by_w, ws_at)
+    oi_ref[:, 0:256] = last_sum(qi, ysi, yri, by_w)
     out = last_sum(qt, yst, yrt, by_z)
-    ot_ref[:, 0:256] = out[0:18, 0:256]
-    oi_ref[:, 256:288] = out[0:18, 256:288]
-    ot_ref[:, 256:288] = pltpu.roll(out[:, 256:384], 96, 1)[0:18, 0:32]
+    ot_ref[:, 0:256] = out[:, 0:256]
+    oi_ref[:, 256:288] = out[:, 256:288]
+    ot_ref[:, 256:288] = pltpu.roll(out[:, 256:384], 96, 1)[:, 0:32]
     for cp in started:
         cp.wait_send()
 
@@ -436,12 +483,14 @@
             vm((2, 4, 64, 384), BF),
             vm((8, 144, 256), BF),
             vm((8, 144, 256), BF),
-            vm((8, 144, 384), BF),
-            vm((8, 144, 384), BF),
-            vm((8, 32, 256), BF),
-            vm((8, 32, 256), BF),
-            vm((8, 32, 384), BF),
-            vm((8, 32, 384), BF),
+            vm((8, 144, 256), BF),
+            vm((8, 144, 256), BF),
+            vm((8, 80, 128), BF),
+            vm((8, 80, 128), BF),
+            vm((8, 16, 384), BF),
+            vm((8, 16, 384), BF),
+            vm((8, 16, 512), BF),
+            vm((8, 16, 512), BF),
             pltpu.SemaphoreType.DMA((4,)),
             pltpu.SemaphoreType.DMA((COPIES,)),
             pltpu.SemaphoreType.DMA((COPIES,)),

time: 94.9 us -> 91.9 us (0.968)
  Pallas kernels: 90.8 us -> 87.7 us
    pallas_call x1, Pallas kernels: 90.8 us -> 87.7 us  [local(): pl.pallas_call(functools.partial(kernel, total), out_shape=(out, out), in...]
where the time goes in v5:
time: 91.9 us; the launch traced here: 91.7 us
  Pallas kernels  87.7 us (95%)
  local copies, waits for them, and re-layouts  2.01 us (2%)
  between operations  1.94 us (2%)
    pallas_call x1, Pallas kernels, local(): pl.pallas_call(functools.partial(kernel, total), out_shape=(out, out), in...  87.7 us
    unnamed x4, local copies, waits for them, and re-layouts  2.01 us

profile of v5, /device:TPU:2, one launch (start us, length us, event | category | flops | bytes accessed | tf_op | source)
XLA Modules:
  0.0 91.7 jit_solution(6443159445266652926)
XLA Ops:
  1.9 87.7 %contrastive.1 = (f32[18,288]{1,0:T(8,128)}, f32[18,288]{1,0:T(8,128)}) custom-call(bf16[224,1152]{1,0:T(8,128)(2,1)} %fi_hbm.1, bf16[224,1152]{1,0:T(8,128)(2,1)} %ft_hbm.1, bf16[288,1152]{1,0:T(8,128)(2,1)} %bitcast.2, bf16[288,1152]{1,0:T(8,128)(2,1)} %bitcast.3, f32[1]{0:T(128)S(6)} %copy.10.lt_ref, f32[1]{0:T(128)S(6)} %copy.11.bs_ref), custom_call_target="tpu_custom_call" | custom-call | tf_op jit(solution)/shard_map/contrastive/pallas_call | solution.py:453
  89.7 0.0 copy-start
  89.7 1.4 %copy.12 = f32[18,288]{1,0:T(8,128)} copy(f32[18,288]{1,0:T(8,128)} %get-tuple-element.4) | data formatting | bytes 41472
  91.1 0.0 copy-done
  91.1 0.6 copy.13
Async XLA Ops:
  89.7 1.4 %copy-start = (f32[18,288]{1,0:T(8,128)S(1)}, f32[18,288]{1,0:T(8,128)}, u32[]{:S(2)}) copy-start(f32[18,288]{1,0:T(8,128)} %get-tuple-element.5) | copy-start | bytes 62212

commit v6 on v5

--- a/solution.py
+++ b/solution.py
@@ -25,11 +25,12 @@
     return lax.dot_general(a, b, (((0,), (0,)), ((), ())), preferred_element_type=F32)
 
 
-def kernel(total, fi_hbm, ft_hbm, wi_hbm, wt_hbm, lt_ref, bs_ref, oi_ref, ot_ref,
-           feats, wts, featst, es, er, unit, scal, img, txt, prob, gi, gt,
-           gib, ra, ra2, r4, sa, sab, gts, sibr, gtb, tr, zs, zr,
+def kernel(total, fi_hbm, ft_hbm, wi_hbm, wt_hbm, lt_ref, bs_ref, o_ref,
+           feats, wts, featst, es, er, esr, err, unit, scal, img, txt, prob, gi, gt,
+           gib, ra, ra2, r2, r4, sa, sab, gts, sibr, gtb, tr, zs, zr, zsr, zrr,
            fsi, fri, fst, frt, fsr, frr, ysi, yri, yst, yrt,
            lsem, ssem, rsem):
+    oi_ref, ot_ref = o_ref.at[0], o_ref.at[1]
     dp, mp = lax.axis_index("dp"), lax.axis_index("mp")
     z, xl, y = dp // 8, (dp // 4) % 2, dp % 4
     c = mp % 2
@@ -69,34 +70,44 @@
         started.append(cp)
         return cp
 
-    place = (lax.broadcasted_iota(jnp.int32, (32, 128), 1)
-             == lax.broadcasted_iota(jnp.int32, (32, 128), 0) + 32 * mp).astype(F32).astype(BF)
-    emb_in = [[], []]
+    l0 = lax.broadcasted_iota(jnp.int32, (32, 128), 0)
+    l1 = lax.broadcasted_iota(jnp.int32, (32, 128), 1)
+    emb_in = []
+    rests = []
     for m in (0, 1):
         loads[2 * m].wait()
         loads[2 * m + 1].wait()
         main = dot_nt(feats[m], wts[m, 0:256, :]).astype(BF)
         rest = dot_nt(feats[m], wts[m, 256:288, :]).astype(BF)
-        rest = dot(rest, place).astype(BF)
+        place = (l1 == l0 + 32 * ((mp + 2 * m) % 4)).astype(F32).astype(BF)
+        rests.append(dot(rest, place))
         for q in range(4):
-            es[m, q, :, 0:256] = main[64 * q:64 * q + 64]
-            es[m, q, :, 256:384] = rest[64 * q:64 * q + 64]
+            es[m, q] = main[64 * q:64 * q + 64]
         if m == 0:
             pl.semaphore_wait(barrier, len(greeted))
-        for k in (1, 2, 3):
-            emb_in[m].append(send(es.at[m, (mp + k) % 4], er.at[m, mp], mps[k - 1]))
+        else:
+            rest = (rests[0] + rests[1]).astype(BF)
+            for q in range(4):
+                esr[q] = rest[64 * q:64 * q + 64]
+            emb_in += [send(esr.at[(mp + k) % 4], err.at[mp], mps[k - 1]) for k in (1, 2, 3)]
+            err[mp] = esr[mp]
+        emb_in += [send(es.at[m, (mp + k) % 4], er.at[m, mp], mps[k - 1]) for k in (1, 2, 3)]
         er[m, mp] = es[m, mp]
 
+    lane = lax.broadcasted_iota(jnp.int32, (64, 128), 1) // 32
+
     def normalize(m):
-        for cp in emb_in[m]:
-            cp.wait_recv()
-        rest = sum(er[m, q, :, 256:384].astype(F32) for q in range(4))
-        wide = jnp.concatenate([er[m, q, :, 0:256].astype(F32) for q in range(4)] + [rest], axis=1)
+        rest = sum(jnp.where(lane == (q + 2 * m) % 4, err[q].astype(F32), 0.0) for q in range(4))
+        if m:
+            rest = pltpu.roll(rest, 64, 1)
+        wide = jnp.concatenate([er[m, q].astype(F32) for q in range(4)] + [rest], axis=1)
         scale = lax.rsqrt(jnp.sum(wide * wide, axis=1, keepdims=True) + 1e-06)
         unit[m] = wide * scale
         scal[m] = jnp.broadcast_to(scale, (64, 128))
         return (wide * scale).astype(BF)
 
+    for cp in emb_in:
+        cp.wait_recv()
     A, B, A0, A1 = pl.ds(0, 32), pl.ds(32, 32), pl.ds(0, 16), pl.ds(16, 16)
     axis1 = ((xp, x2, xm), (yp, y2, ym))
     axis2 = ((yp, y2, ym), (xp, x2, xm))
@@ -163,10 +174,8 @@
         return logits
 
     def some_scores(k, count):
-        def one(i, _):
+        for i in range(count):
             scores(k, 3 - i)
-            return 0
-        lax.fori_loop(0, count, one, 0)
 
     sent = {}
 
@@ -213,15 +222,9 @@
     third(2)
     text_hop(3, (0,))
 
-    def two_scores(k):
-        def one(i, _):
-            scores(k, 3 - i)
-            return 0
-        lax.fori_loop(0, 2, one, 0)
-
-    two_scores(1)
+    some_scores(1, 2)
     text_hop(3, (1,))
-    two_scores(3)
+    some_scores(3, 2)
     tgot[4, 0].wait_recv()
     tgot[4, 1].wait_recv()
     text_share(4)
@@ -283,11 +286,25 @@
         for j in (2, 3) if n == 0 else (1, 0):
             for h in (0, 1):
                 part = gi[0, h, j] + ra[0, h, j].astype(F32) + ra[1, h, j].astype(F32)
-                if j:
-                    sab[h, j - 1] = part.astype(BF)
-                    qa2.append(send(sab.at[h, j - 1], ra2.at[h, j - 1], axis1[h][j - 1]))
+                if j == 2:
+                    sab[h, 1] = part.astype(BF)
+                    q2h.append(send(sab.at[h, 1, A0], r2.at[h, A0], axis1[h][0]))
+                    q2h.append(send(sab.at[h, 1, A1], r2.at[h, A1], axis1[h][2]))
                 else:
-                    sa[h] = part
+                    sa[h, j] = part
+
+    q2h = []
+
+    def image_last():
+        for h in (0, 1):
+            for cp in q2h[2 * h:2 * h + 2]:
+                cp.wait_recv()
+            sab[h, 0, A0] = (sa[h, 1, A0] + r2[h, A0].astype(F32)).astype(BF)
+            sab[h, 0, A1] = sa[h, 1, A1].astype(BF)
+            sab[h, 2, A0] = sa[h, 3, A0].astype(BF)
+            sab[h, 2, A1] = (sa[h, 3, A1] + r2[h, A1].astype(F32)).astype(BF)
+            qa2.append(send(sab.at[h, 0], ra2.at[h, 0], axis1[h][0]))
+            qa2.append(send(sab.at[h, 2], ra2.at[h, 1], axis1[h][2]))
 
     image_on(0)
     q2 = text_block(2)
@@ -306,27 +323,33 @@
     text_on(1, 1)
     text_on(7, 0)
     image_first(1)
+    image_last()
     text_on(1, 0)
     text_on(7, 1)
 
     def back(m, dx):
         inner = jnp.sum(unit[m] * dx, axis=1, keepdims=True)
-        dz = (scal[m][:, 0:1] * (dx - unit[m] * inner)).astype(BF)
+        dz = scal[m][:, 0:1] * (dx - unit[m] * inner)
         for q in range(4):
-            zs[m, q, :, 0:256] = dz[:, 256 * q:256 * q + 256]
-            zs[m, q, :, 256:384] = dz[:, 1024:1152]
+            zs[m, q] = dz[:, 256 * q:256 * q + 256].astype(BF)
         zr[m, mp] = zs[m, mp]
-        return [send(zs.at[m, (mp + k) % 4], zr.at[m, mp], mps[k - 1]) for k in (1, 2, 3)]
+        return dz[:, 1024:1152], [send(zs.at[m, (mp + k) % 4], zr.at[m, mp], mps[k - 1]) for k in (1, 2, 3)]
 
     for k in (1, 7):
         for half in (0, 1):
             sent[k, half].wait_recv()
-    zt_in = back(1, text_own(0) + tr[1].astype(F32) + tr[7].astype(F32))
+    rest_t, z_in = back(1, text_own(0) + tr[1].astype(F32) + tr[7].astype(F32))
     for cp in qa2:
         cp.wait_recv()
-    zi_in = back(0, jnp.concatenate(
-        [sa[h] + ra2[h, 0].astype(F32) + ra2[h, 1].astype(F32) + ra2[h, 2].astype(F32)
+    rest_i, q = back(0, jnp.concatenate(
+        [sa[h, 0] + ra2[h, 0].astype(F32) + ra2[h, 1].astype(F32)
          for h in (0, 1)], axis=0))
+    z_in += q
+    for q in range(4):
+        turned = [pltpu.roll(r, (128 - 32 * q + 32 * m) % 128, 1) for m, r in ((0, rest_i), (1, rest_t))]
+        zsr[q] = jnp.where(lane == 0, turned[0], turned[1]).astype(BF)
+    zrr[mp] = zsr[mp]
+    z_in += [send(zsr.at[(mp + k) % 4], zrr.at[mp], mps[k - 1]) for k in (1, 2, 3)]
 
     wide_t = jnp.transpose(feats[0])
     for k in range(8):
@@ -344,22 +367,14 @@
 
 
     far_z, far_w = (4, 3, 5, 2, 6, 1, 7), (6, 2, 5, 7, 1, 3, 4)
-    l0 = lax.broadcasted_iota(jnp.int32, (128, 128), 0)
-    l1 = lax.broadcasted_iota(jnp.int32, (128, 128), 1)
-
     def by_z(k):
         return (z + k) % 8
 
     def by_w(k):
         return ((xl + k // 4) % 2) * 4 + (y + k) % 4
 
-    def columns(m, arrived):
-        for cp in arrived:
-            cp.wait_recv()
-        pick = ((l0 + 32 * m == l1 + 32 * mp) & (l1 >= 32 * m) & (l1 < 32 * m + 32)).astype(F32).astype(BF)
-        rest = jnp.concatenate([zr[m, q, :, 256:384] for q in range(4)], axis=0)
-        return (jnp.concatenate([zr[m, q, :, 0:256] for q in range(4)], axis=0),
-                dot(rest, pick).astype(BF))
+    def rows(ref):
+        return jnp.concatenate([ref[q] for q in range(4)], axis=0)
 
     def regroup(q, own, rc, near, far, ys, yr, base, at):
         for cp in q:
@@ -385,14 +400,33 @@
         tail = [jnp.concatenate([out[r * n + i:r * n + i + 1, cols:] for i in range(n)], axis=1) for r in (0, 1)]
         return jnp.concatenate([out[:, 0:cols]] + tail, axis=0)
 
-    main_i, rest_i = columns(0, zi_in)
-    main_t, rest_t = columns(1, zt_in)
+    for cp in z_in:
+        cp.wait_recv()
+    main_i, main_t = rows(zr.at[0]), rows(zr.at[1])
+    rest = rows(zrr).astype(F32)
+    which = lax.broadcasted_iota(jnp.int32, (256, 128), 1) // 32
+    rest_i = jnp.where(which == 0, rest, 0.0).astype(BF)
+    rest_t = jnp.where(which == 1, rest, 0.0).astype(BF)
 
     def make_t(k):
         a, b = featst[1, by_w(k)], featst[2, by_w(k)]
         rest = dot(a, rest_t) + dot(b, rest_i)
         return dot(a, main_t), rest[0:72] + pltpu.roll(rest[72:144], 64, 1)
 
+    def make_i(k):
+        return dot(featst[0, by_z(k)], main_i)
+
+    H0, H1 = pl.ds(0, 80), pl.ds(80, 64)
+    fsi[4] = make_i(4).astype(BF)
+    qi4 = [send(fsi.at[4, H0], fri.at[4, H0], zs_at[2]), send(fsi.at[4, H1], fri.at[4, H1], zs_at[6])]
+    qi3, qi = [], []
+
+    def to_next(k, q):
+        fsi[k] = make_i(k).astype(BF)
+        q.append(send(fsi.at[k], fri.at[k], zp if k < 4 else zm))
+
+    to_next(3, qi3)
+    to_next(5, qi3)
     qt = []
     for k in far_w:
         part, rest = make_t(k)
@@ -403,16 +437,8 @@
     own_t, own_r = make_t(0)
 
 
-    def make_i(k):
-        return dot(featst[0, by_z(k)], main_i)
-
-    H0, H1 = pl.ds(0, 80), pl.ds(80, 64)
-    fsi[4] = make_i(4).astype(BF)
-    qi4 = [send(fsi.at[4, H0], fri.at[4, H0], zs_at[2]), send(fsi.at[4, H1], fri.at[4, H1], zs_at[6])]
-    qi3, qi = [], []
-    for k, q in ((3, qi3), (5, qi3), (1, qi), (7, qi)):
-        fsi[k] = make_i(k).astype(BF)
-        q.append(send(fsi.at[k], fri.at[k], zp if k < 4 else zm))
+    to_next(1, qi)
+    to_next(7, qi)
     own_2, own_6 = make_i(2), make_i(6)
     own_i = make_i(0)
     for k, part, via, half in ((2, own_2, 3, 0), (6, own_6, 5, 1)):
@@ -450,18 +476,20 @@
     total = image_feats.shape[0] * lax.axis_size("dp")
     vm = pltpu.VMEM
     out = jax.ShapeDtypeStruct((18, 288), F32)
-    return pl.pallas_call(
+    res = pl.pallas_call(
         functools.partial(kernel, total),
-        out_shape=(out, out),
+        out_shape=jax.ShapeDtypeStruct((2, 18, 288), F32),
         in_specs=[pl.BlockSpec(memory_space=pl.ANY)] * 4
         + [pl.BlockSpec(memory_space=pltpu.SMEM)] * 2,
-        out_specs=(pl.BlockSpec(memory_space=vm), pl.BlockSpec(memory_space=vm)),
+        out_specs=pl.BlockSpec(memory_space=vm),
         scratch_shapes=[
             vm((2, 256, 1152), BF),
             vm((2, 288, 1152), BF),
             vm((3, 8, 144, 256), BF),
-            vm((2, 4, 64, 384), BF),
-            vm((2, 4, 64, 384), BF),
+            vm((2, 4, 64, 256), BF),
+            vm((2, 4, 64, 256), BF),
+            vm((4, 64, 128), BF),
+            vm((4, 64, 128), BF),
             vm((2, 64, 1152), F32),
             vm((2, 64, 128), F32),
             vm((4, 2, 4, 32, 1152), BF),
@@ -471,16 +499,19 @@
             vm((8, 2, 64, 1152), F32),
             vm((3, 2, 4, 32, 1152), BF),
             vm((2, 2, 4, 32, 1152), BF),
-            vm((2, 3, 32, 1152), BF),
+            vm((2, 2, 32, 1152), BF),
+            vm((2, 32, 1152), BF),
             vm((2, 4, 32, 1152), BF),
-            vm((2, 32, 1152), F32),
+            vm((2, 4, 32, 1152), F32),
             vm((2, 3, 32, 1152), BF),
             vm((4, 2, 64, 1152), BF),
             vm((4, 2, 64, 1152), BF),
             vm((8, 64, 1152), BF),
             vm((8, 64, 1152), BF),
-            vm((2, 4, 64, 384), BF),
-            vm((2, 4, 64, 384), BF),
+            vm((2, 4, 64, 256), BF),
+            vm((2, 4, 64, 256), BF),
+            vm((4, 64, 128), BF),
+            vm((4, 64, 128), BF),
             vm((8, 144, 256), BF),
             vm((8, 144, 256), BF),
             vm((8, 144, 256), BF),
@@ -500,6 +531,7 @@
             collective_id=0, has_side_effects=True, vmem_limit_bytes=60 * 2**20
         ),
     )(image_feats, text_feats, image_proj.T, text_proj.T, log_temp, bias)
+    return res[0], res[1]
 
 
 def solution(mesh):

time: 91.9 us -> 88.5 us (0.963); the launches traced: 91.7 us -> 87.3 us
  Pallas kernels: 87.7 us -> 83.9 us
    pallas_call x1, Pallas kernels: 87.7 us -> 83.9 us  [local(): pl.pallas_call(functools.partial(kernel, total), out_shape=jax.ShapeDtype...]
    unnamed x4 -> x0, local copies, waits for them, and re-layouts: 2.01 us -> none
    squeeze x0 -> x1, local copies, waits for them, and re-layouts: none -> 1.42 us  [local(): return (res[0], res[1])]
where the time goes in v6:
time: 88.5 us; the launch traced here: 87.3 us
  Pallas kernels  83.9 us (95%)
  between operations  1.93 us (2%)
  local copies, waits for them, and re-layouts  1.42 us (2%)
    pallas_call x1, Pallas kernels, local(): pl.pallas_call(functools.partial(kernel, total), out_shape=jax.ShapeDtype...  83.9 us

profile of v6, /device:TPU:2, one launch (start us, length us, event | category | flops | bytes accessed | tf_op | source)
XLA Modules:
  0.0 87.3 jit_solution(3503476344004178891)
XLA Ops:
  1.9 83.9 %contrastive.1 = f32[2,18,288]{2,1,0:T(8,128)} custom-call(bf16[224,1152]{1,0:T(8,128)(2,1)} %fi_hbm.1, bf16[224,1152]{1,0:T(8,128)(2,1)} %ft_hbm.1, bf16[288,1152]{1,0:T(8,128)(2,1)} %bitcast.6, bf16[288,1152]{1,0:T(8,128)(2,1)} %bitcast.7, f32[1]{0:T(128)S(6)} %copy.8.lt_ref, f32[1]{0:T(128)S(6)} %copy.9.bs_ref), custom_call_target="tpu_custom_call" | custom-call | tf_op jit(solution)/shard_map/contrastive/pallas_call | solution.py:479
  85.9 1.4 %slice_bitcast_fusion = (f32[18,288]{1,0:T(8,128)}, f32[18,288]{1,0:T(8,128)}) fusion(f32[2,18,288]{2,1,0:T(8,128)} %contrastive.1), kind=kLoop, calls=%fused_computation | loop fusion | bytes 82944 | tf_op jit(solution)/shard_map/squeeze | solution.py:534

commit v7 on v6

--- a/solution.py
+++ b/solution.py
@@ -60,7 +60,7 @@
         loads.append(cp)
     feats[:, 224:256, :] = jnp.zeros((2, 32, 1152), BF)
 
-    started = []
+    started, gone = [], []
 
     def send(src, dst, to):
         k = len(started)
@@ -159,9 +159,12 @@
 
     text_send(0, 7, 0, zp)
     text_send(0, 1, 1, zm)
+    text_share(0)
+    for cp in (tgot[7, 0], tgot[1, 1]):
+        cp.wait_send()
+        gone.append(cp)
     text_send(0, 7, 1, zp)
     text_send(0, 1, 0, zm)
-    text_share(0)
     temp = jnp.exp(jnp.full((1, 1), lt_ref[0], F32))
     shift = jnp.full((1, 1), bs_ref[0], F32)
     gain = temp * (1.0 / total)
@@ -203,37 +206,45 @@
         to = zp if k < 4 or (k == 4 and half == 0) else zm
         sent[k, half] = send(gtb.at[k, at], tr.at[k, at], to)
 
+    text_hop(1, (0,))
     for j in (1, 3):
         got[0, 0, j].wait_recv()
         got[0, 1, j].wait_recv()
         second(j)
-    text_hop(1)
+    text_hop(1, (1,))
     got[0, 0, 2].wait_recv()
     got[0, 1, 2].wait_recv()
     second(2)
+    text_hop(2, (0,))
     third(0)
-    text_hop(2)
+    text_hop(2, (1,))
     text_shared(1, 7)
     scores(0, 3)
     third(1)
     third(3)
+    text_hop(3, (0,))
     text_shared(2, 6)
     scores(0, 2)
     third(2)
-    text_hop(3, (0,))
 
     some_scores(1, 2)
     text_hop(3, (1,))
     some_scores(3, 2)
+    text_shared(3, 5, 0)
+    scores(1, 1)
+    scores(3, 1)
     tgot[4, 0].wait_recv()
     tgot[4, 1].wait_recv()
     text_share(4)
-    text_shared(3, 5, 0)
-    for k in (1, 3, 0):
-        scores(k, 1)
+    scores(0, 1)
+    for j in range(4):
+        for h in (0, 1):
+            got[4, h, j].wait_recv()
+            got[5, h, j].wait_recv()
+    some_scores(2, 3)
     text_shared(4)
-    scores(1, 0)
-    scores(3, 0)
+    for k in (2, 1, 3):
+        scores(k, 0)
     logits = scores(0, 0)
     r0 = lax.broadcasted_iota(jnp.int32, (32, 128), 0)
     r1 = lax.broadcasted_iota(jnp.int32, (32, 128), 1)
@@ -242,11 +253,6 @@
         prob[128 * h:128 * h + 32, 128:256] = jnp.where(
             r1 == r0 + 32 * h, -gain / (1.0 + jnp.exp(own)), gain / (1.0 + jnp.exp(-own))).astype(BF)
 
-    for j in range(4):
-        for h in (0, 1):
-            got[4, h, j].wait_recv()
-            got[5, h, j].wait_recv()
-    some_scores(2, 4)
     q0 = text_block(0)
     image_block(2)
     gib[1] = gi[2].astype(BF)
@@ -323,9 +329,9 @@
     text_on(1, 1)
     text_on(7, 0)
     image_first(1)
-    image_last()
     text_on(1, 0)
     text_on(7, 1)
+    image_last()
 
     def back(m, dx):
         inner = jnp.sum(unit[m] * dx, axis=1, keepdims=True)
@@ -466,7 +472,8 @@
     oi_ref[:, 256:288] = out[:, 256:288]
     ot_ref[:, 256:288] = pltpu.roll(out[:, 256:384], 96, 1)[:, 0:32]
     for cp in started:
-        cp.wait_send()
+        if not any(cp is g for g in gone):
+            cp.wait_send()
 
 
 COPIES = 256
@@ -475,7 +482,6 @@
 def local(image_feats, text_feats, image_proj, text_proj, log_temp, bias):
     total = image_feats.shape[0] * lax.axis_size("dp")
     vm = pltpu.VMEM
-    out = jax.ShapeDtypeStruct((18, 288), F32)
     res = pl.pallas_call(
         functools.partial(kernel, total),
         out_shape=jax.ShapeDtypeStruct((2, 18, 288), F32),

time: 88.5 us -> 85.1 us (0.962)
  Pallas kernels: 83.9 us -> 81.2 us
    pallas_call x1, Pallas kernels: 83.9 us -> 81.2 us  [local(): pl.pallas_call(functools.partial(kernel, total), out_shape=jax.ShapeDtype...]
where the time goes in v7:
time: 85.1 us; the launch traced here: 84.6 us
  Pallas kernels  81.2 us (95%)
  between operations  1.93 us (2%)
  local copies, waits for them, and re-layouts  1.42 us (2%)
    pallas_call x1, Pallas kernels, local(): pl.pallas_call(functools.partial(kernel, total), out_shape=jax.ShapeDtype...  81.2 us

profile of v7, /device:TPU:2, one launch (start us, length us, event | category | flops | bytes accessed | tf_op | source)
XLA Modules:
  0.0 84.6 jit_solution(15334248541533715186)
XLA Ops:
  1.9 81.2 %contrastive.1 = f32[2,18,288]{2,1,0:T(8,128)} custom-call(bf16[224,1152]{1,0:T(8,128)(2,1)} %fi_hbm.1, bf16[224,1152]{1,0:T(8,128)(2,1)} %ft_hbm.1, bf16[288,1152]{1,0:T(8,128)(2,1)} %bitcast.6, bf16[288,1152]{1,0:T(8,128)(2,1)} %bitcast.7, f32[1]{0:T(128)S(6)} %copy.8.lt_ref, f32[1]{0:T(128)S(6)} %copy.9.bs_ref), custom_call_target="tpu_custom_call" | custom-call | tf_op jit(solution)/shard_map/contrastive/pallas_call | solution.py:485
  83.1 1.4 %slice_bitcast_fusion = (f32[18,288]{1,0:T(8,128)}, f32[18,288]{1,0:T(8,128)}) fusion(f32[2,18,288]{2,1,0:T(8,128)} %contrastive.1), kind=kLoop, calls=%fused_computation | loop fusion | bytes 82944 | tf_op jit(solution)/shard_map/squeeze | solution.py:540

commit v8 on v7

--- a/solution.py
+++ b/solution.py
@@ -47,17 +47,17 @@
     sib = (dp, (mp // 2) * 2 + (1 - c))
     mps = [(dp, (mp + k) % 4) for k in (1, 2, 3)]
 
-    barrier = pltpu.get_barrier_semaphore()
-    greeted = mps + [xp, xm] + zs_at[1:] + ws_at[1:4] + ws_at[5:]
-    for d in greeted:
-        pl.semaphore_signal(barrier, inc=1, device_id=d, device_id_type=MESH)
-
     loads = []
     for k, (s, t) in enumerate(((fi_hbm, feats.at[0, 0:224]), (wi_hbm, wts.at[0]),
                                 (ft_hbm, feats.at[1, 0:224]), (wt_hbm, wts.at[1]))):
         cp = pltpu.make_async_copy(s, t, lsem.at[k])
         cp.start()
         loads.append(cp)
+    barrier = pltpu.get_barrier_semaphore()
+    greeted = mps + [xp, xm] + zs_at[1:] + ws_at[1:4] + ws_at[5:]
+    for d in greeted:
+        pl.semaphore_signal(barrier, inc=1, device_id=d, device_id_type=MESH)
+
     feats[:, 224:256, :] = jnp.zeros((2, 32, 1152), BF)
 
     started, gone = [], []
@@ -257,9 +257,13 @@
     image_block(2)
     gib[1] = gi[2].astype(BF)
     pairs = (pl.ds(2, 2), pl.ds(0, 2))
-    q4 = [[[send(gib.at[1, h, p, A0], r4.at[h, p, A0], axis2[h][0]),
-            send(gib.at[1, h, p, A1], r4.at[h, p, A1], axis2[h][2])] for h in (0, 1)] for p in pairs]
+    def two_away(p):
+        return [[send(gib.at[1, h, p, A0], r4.at[h, p, A0], axis2[h][0]),
+                 send(gib.at[1, h, p, A1], r4.at[h, p, A1], axis2[h][2])] for h in (0, 1)]
+
+    q4 = [two_away(pairs[0])]
     q1 = text_block(1)
+    q4.append(two_away(pairs[1]))
     q0.wait_recv()
     text_on(4, 0)
     text_on(4, 1)
@@ -464,10 +468,27 @@
         own_r = own_r + frr[k, 0:72].astype(F32)
         own_t = own_t + frt[k].astype(F32)
     own_t = jnp.concatenate([own_t, jnp.concatenate([own_r, pltpu.roll(own_r, 64, 1)], axis=0)], axis=1)
-    qt = regroup([], own_t, frt, (), far_z, yst, yrt, by_z, zs_at)
+    low = lax.broadcasted_iota(jnp.int32, (16, 128), 1) < 64
+    for k in range(8):
+        part = own_t[18 * k:18 * k + 18]
+        tail = jnp.concatenate([part[r:r + 1, i:i + 128] for r in (16, 17) for i in (0, 128, 256)]
+                               + [jnp.zeros((2, 128), F32)], axis=0)
+        tail = jnp.concatenate([pltpu.roll(tail, 64, 1), tail[0:2], tail[3:5], jnp.zeros((4, 128), F32)], axis=0)
+        yst[k, :, 0:256] = part[0:16, 0:256].astype(BF)
+        yst[k, :, 256:384] = jnp.where(low, part[0:16, 256:384], tail).astype(BF)
+    qt = [send(yst.at[by_z(k)], yrt.at[k], zs_at[k]) for k in far_z]
     qi = regroup(qi, own_i, fri, (1, 7, 2, 6), far_w, ysi, yri, by_w, ws_at)
     oi_ref[:, 0:256] = last_sum(qi, ysi, yri, by_w)
-    out = last_sum(qt, yst, yrt, by_z)
+    for cp in qt:
+        cp.wait_recv()
+    out = yst[by_z(0)].astype(F32)
+    for k in range(1, 8):
+        out = out + yrt[k].astype(F32)
+    rest = out[:, 256:384]
+    turned = pltpu.roll(rest, 64, 1)
+    tail = [jnp.concatenate([jnp.where(low[0:1], turned[3 * r + i:3 * r + i + 1], rest[8 + 2 * r + i:9 + 2 * r + i])
+                             for i in (0, 1)] + [turned[3 * r + 2:3 * r + 3]], axis=1) for r in (0, 1)]
+    out = jnp.concatenate([out] + tail, axis=0)
     ot_ref[:, 0:256] = out[:, 0:256]
     oi_ref[:, 256:288] = out[:, 256:288]
     ot_ref[:, 256:288] = pltpu.roll(out[:, 256:384], 96, 1)[:, 0:32]
@@ -526,8 +547,8 @@
             vm((8, 80, 128), BF),
             vm((8, 16, 384), BF),
             vm((8, 16, 384), BF),
-            vm((8, 16, 512), BF),
-            vm((8, 16, 512), BF),
+            vm((8, 16, 384), BF),
+            vm((8, 16, 384), BF),
             pltpu.SemaphoreType.DMA((4,)),
             pltpu.SemaphoreType.DMA((COPIES,)),
             pltpu.SemaphoreType.DMA((COPIES,)),

time: 85.1 us -> 85.1 us (level)
  no operation moved by 1% of the time
where the time goes in v8:
time: 85.1 us; the launch traced here: 84.1 us
  Pallas kernels  80.7 us (95%)
  between operations  1.93 us (2%)
  local copies, waits for them, and re-layouts  1.42 us (2%)
    pallas_call x1, Pallas kernels, local(): pl.pallas_call(functools.partial(kernel, total), out_shape=jax.ShapeDtype...  80.7 us

profile of v8, /device:TPU:2, one launch (start us, length us, event | category | flops | bytes accessed | tf_op | source)
XLA Modules:
  0.0 84.1 jit_solution(973501411305597557)
XLA Ops:
  1.9 80.7 %contrastive.1 = f32[2,18,288]{2,1,0:T(8,128)} custom-call(bf16[224,1152]{1,0:T(8,128)(2,1)} %fi_hbm.1, bf16[224,1152]{1,0:T(8,128)(2,1)} %ft_hbm.1, bf16[288,1152]{1,0:T(8,128)(2,1)} %bitcast.6, bf16[288,1152]{1,0:T(8,128)(2,1)} %bitcast.7, f32[1]{0:T(128)S(6)} %copy.8.lt_ref, f32[1]{0:T(128)S(6)} %copy.9.bs_ref), custom_call_target="tpu_custom_call" | custom-call | tf_op jit(solution)/shard_map/contrastive/pallas_call | solution.py:506
  82.7 1.4 %slice_bitcast_fusion = (f32[18,288]{1,0:T(8,128)}, f32[18,288]{1,0:T(8,128)}) fusion(f32[2,18,288]{2,1,0:T(8,128)} %contrastive.1), kind=kLoop, calls=%fused_computation | loop fusion | bytes 82944 | tf_op jit(solution)/shard_map/squeeze | solution.py:561

commit v9 on v8

--- a/solution.py
+++ b/solution.py
@@ -441,7 +441,7 @@
     for k in far_w:
         part, rest = make_t(k)
         fst[k] = part.astype(BF)
-        fsr[k, 0:72] = rest.astype(BF)
+        fsr[k] = jnp.concatenate([rest, jnp.zeros((8, 128), F32)], axis=0).astype(BF)
         qt.append(send(fst.at[k], frt.at[k], ws_at[k]))
         qt.append(send(fsr.at[k], frr.at[k], ws_at[k]))
     own_t, own_r = make_t(0)
@@ -465,7 +465,7 @@
     for cp in qt:
         cp.wait_recv()
     for k in far_w:
-        own_r = own_r + frr[k, 0:72].astype(F32)
+        own_r = own_r + frr[k].astype(F32)[0:72]
         own_t = own_t + frt[k].astype(F32)
     own_t = jnp.concatenate([own_t, jnp.concatenate([own_r, pltpu.roll(own_r, 64, 1)], axis=0)], axis=1)
     low = lax.broadcasted_iota(jnp.int32, (16, 128), 1) < 64

time: 85.1 us -> 85.1 us (level)
  no operation moved by 1% of the time
where the time goes in v9:
time: 85.1 us; the launch traced here: 84.1 us
  Pallas kernels  80.7 us (95%)
  between operations  1.93 us (2%)
  local copies, waits for them, and re-layouts  1.42 us (2%)
    pallas_call x1, Pallas kernels, local(): pl.pallas_call(functools.partial(kernel, total), out_shape=jax.ShapeDtype...  80.7 us

profile of v9, /device:TPU:2, one launch (start us, length us, event | category | flops | bytes accessed | tf_op | source)
XLA Modules:
  0.0 84.1 jit_solution(11773339324465236985)
XLA Ops:
  1.9 80.7 %contrastive.1 = f32[2,18,288]{2,1,0:T(8,128)} custom-call(bf16[224,1152]{1,0:T(8,128)(2,1)} %fi_hbm.1, bf16[224,1152]{1,0:T(8,128)(2,1)} %ft_hbm.1, bf16[288,1152]{1,0:T(8,128)(2,1)} %bitcast.6, bf16[288,1152]{1,0:T(8,128)(2,1)} %bitcast.7, f32[1]{0:T(128)S(6)} %copy.8.lt_ref, f32[1]{0:T(128)S(6)} %copy.9.bs_ref), custom_call_target="tpu_custom_call" | custom-call | tf_op jit(solution)/shard_map/contrastive/pallas_call | solution.py:506
  82.7 1.4 %slice_bitcast_fusion = (f32[18,288]{1,0:T(8,128)}, f32[18,288]{1,0:T(8,128)}) fusion(f32[2,18,288]{2,1,0:T(8,128)} %contrastive.1), kind=kLoop, calls=%fused_computation | loop fusion | bytes 82944 | tf_op jit(solution)/shard_map/squeeze | solution.py:561

commit v10 on v9

--- a/solution.py
+++ b/solution.py
@@ -419,9 +419,11 @@
     rest_t = jnp.where(which == 1, rest, 0.0).astype(BF)
 
     def make_t(k):
-        a, b = featst[1, by_w(k)], featst[2, by_w(k)]
-        rest = dot(a, rest_t) + dot(b, rest_i)
-        return dot(a, main_t), rest[0:72] + pltpu.roll(rest[72:144], 64, 1)
+        return dot(featst[1, by_w(k)], main_t)
+
+    def make_r(k):
+        rest = dot(featst[1, by_w(k)], rest_t) + dot(featst[2, by_w(k)], rest_i)
+        return rest[0:72] + pltpu.roll(rest[72:144], 64, 1)
 
     def make_i(k):
         return dot(featst[0, by_z(k)], main_i)
@@ -438,13 +440,13 @@
     to_next(3, qi3)
     to_next(5, qi3)
     qt = []
-    for k in far_w:
-        part, rest = make_t(k)
-        fst[k] = part.astype(BF)
-        fsr[k] = jnp.concatenate([rest, jnp.zeros((8, 128), F32)], axis=0).astype(BF)
+    for k in (6, 5, 7, 4, 2, 1, 3):
+        fst[k] = make_t(k).astype(BF)
         qt.append(send(fst.at[k], frt.at[k], ws_at[k]))
+    for k in (6, 5, 7, 4, 2, 1, 3):
+        fsr[k] = jnp.concatenate([make_r(k), jnp.zeros((8, 128), F32)], axis=0).astype(BF)
         qt.append(send(fsr.at[k], frr.at[k], ws_at[k]))
-    own_t, own_r = make_t(0)
+    own_t, own_r = make_t(0), make_r(0)
 
 
     to_next(1, qi)

time: 85.1 us -> 85.2 us (level)
  no operation moved by 1% of the time
where the time goes in v10:
time: 85.2 us; the launch traced here: 84.3 us
  Pallas kernels  81 us (95%)
  between operations  1.93 us (2%)
  local copies, waits for them, and re-layouts  1.42 us (2%)
    pallas_call x1, Pallas kernels, local(): pl.pallas_call(functools.partial(kernel, total), out_shape=jax.ShapeDtype...  81 us

profile of v10, /device:TPU:2, one launch (start us, length us, event | category | flops | bytes accessed | tf_op | source)
XLA Modules:
  0.0 84.3 jit_solution(3293296569942879145)
XLA Ops:
  1.9 81.0 %contrastive.1 = f32[2,18,288]{2,1,0:T(8,128)} custom-call(bf16[224,1152]{1,0:T(8,128)(2,1)} %fi_hbm.1, bf16[224,1152]{1,0:T(8,128)(2,1)} %ft_hbm.1, bf16[288,1152]{1,0:T(8,128)(2,1)} %bitcast.6, bf16[288,1152]{1,0:T(8,128)(2,1)} %bitcast.7, f32[1]{0:T(128)S(6)} %copy.8.lt_ref, f32[1]{0:T(128)S(6)} %copy.9.bs_ref), custom_call_target="tpu_custom_call" | custom-call | tf_op jit(solution)/shard_map/contrastive/pallas_call | solution.py:508
  82.9 1.4 %slice_bitcast_fusion = (f32[18,288]{1,0:T(8,128)}, f32[18,288]{1,0:T(8,128)}) fusion(f32[2,18,288]{2,1,0:T(8,128)} %contrastive.1), kind=kLoop, calls=%fused_computation | loop fusion | bytes 82944 | tf_op jit(solution)/shard_map/squeeze | solution.py:563
